TPU v7x, 512 devices: a whole 4x8x8 slice. The times are simulated.
512 devices in a mesh: ctx: 8 (over z), exp: 16 (over y_hi, x), rep: 4 (over y_lo, core).
Axes of the slice: x: 4, y: 8 (y_hi: 4, y_lo: 2; y = y_hi * 2 + y_lo), z: 8, core: 2. Of those that a mesh axis runs over, the one named last changes fastest.
Arguments:
- acts: bfloat16 [4096, 2048], P(('ctx', 'exp'), 'rep'), may hold values from -6 to 6
- grad_out: bfloat16 [4096, 2048], P(('ctx', 'exp'), 'rep'), may hold values from -0.59765625 to 0.59765625
- experts_idx: int32 [4096, 8], P(('ctx', 'exp')), may hold values from 0 to 127, all different within a row; in each aligned block of 32 rows (0 to 31, 32 to 63, ...) at most 3 rows name the same one
- gate_prob: bfloat16 [4096, 8], P(('ctx', 'exp')), may hold values from 0.049804688 to 1
- w_gate: bfloat16 [128, 768, 2048], P(('ctx', 'exp'), 'rep'), may hold values from -0.125 to 0.125
- w_up: bfloat16 [128, 768, 2048], P(('ctx', 'exp'), 'rep'), may hold values from -0.125 to 0.125
- w_down: bfloat16 [128, 768, 2048], P(('ctx', 'exp'), 'rep'), may hold values from -0.21875 to 0.21875
Outputs:
- acts_grad: bfloat16 [4096, 2048], P(('ctx', 'exp'), 'rep')
- gate_grad_tok: bfloat16 [4096, 8], P(('ctx', 'exp'))
- w_gate_grad: bfloat16 [128, 768, 2048], P(('ctx', 'exp'), 'rep')
- w_up_grad: bfloat16 [128, 768, 2048], P(('ctx', 'exp'), 'rep')
- w_down_grad: bfloat16 [128, 768, 2048], P(('ctx', 'exp'), 'rep')
Inputs may be any that keep to these rules, and one draw needn't show every extreme that they name: `experts_idx`: each row names 8 different experts. Within the rows of one index of ctx+exp (32 aligned rows), no expert is named by more than 3 rows, a bound that some block reaches.
All inputs are finite; a program needn't handle non-finite values.
Results may differ from a plain program's by a relative error of at most 0.012.
Values may be sent and summed in bfloat16 or wider, within the bound.
No kernel may reach another device: no remote copies, remote signals or barrier semaphores. Data moves between devices by JAX's collectives and lax.ppermute only.
A program may use at most 64 MiB of HBM per device.

v0:
```python
import jax
import jax.numpy as jnp
from jax import lax
from jax.sharding import PartitionSpec as P


def slot_tables(experts_idx, expert_count, capacity):
    tokens_here, top_count = experts_idx.shape
    labels = jnp.arange(expert_count, dtype=jnp.int32)
    picked = (experts_idx[:, :, None] == labels[None, None, :]).astype(jnp.int32)
    flat_pick = picked.reshape(tokens_here * top_count, expert_count)
    earlier = jnp.cumsum(flat_pick, axis=0) - flat_pick
    slot_number = jnp.sum(flat_pick * (labels[None, :] * capacity + earlier), axis=1)
    slot_labels = jnp.arange(expert_count * capacity, dtype=jnp.int32)
    select = (slot_number[None, :] == slot_labels[:, None]).astype(jnp.bfloat16)
    placing = jnp.sum(select.reshape(expert_count * capacity, tokens_here, top_count), axis=2)
    return (select, placing)


def body(acts, grad_out, experts_idx, gate_prob, w_gate, w_up, w_down):
    tokens_here, top_count = experts_idx.shape
    expert_count = lax.axis_size(("ctx", "exp"))
    capacity = min(tokens_here, 3 * tokens_here * top_count // (2 * expert_count))
    select, placing = slot_tables(experts_idx, expert_count, capacity)
    slot_gate = jnp.dot(select, gate_prob.reshape(-1), preferred_element_type=jnp.float32).astype(
        jnp.bfloat16
    )
    full_acts, full_grad = (
        lax.all_gather(acts, "rep", axis=1, tiled=True),
        lax.all_gather(grad_out, "rep", axis=1, tiled=True),
    )
    send_acts = jnp.dot(placing, full_acts, preferred_element_type=jnp.float32).astype(jnp.bfloat16)
    send_grad = jnp.dot(placing, full_grad, preferred_element_type=jnp.float32).astype(jnp.bfloat16)
    rows_acts, rows_grad, rows_gate = (
        lax.all_to_all(send_acts, ("ctx", "exp"), split_axis=0, concat_axis=0, tiled=True),
        lax.all_to_all(send_grad, ("ctx", "exp"), split_axis=0, concat_axis=0, tiled=True),
        lax.all_to_all(slot_gate, ("ctx", "exp"), split_axis=0, concat_axis=0, tiled=True),
    )
    gate_w = w_gate[0]
    up_w = w_up[0]
    down_w = w_down[0]
    contract_last = (((1,), (1,)), ((), ()))
    contract_first = (((0,), (0,)), ((), ()))
    pre_gate = lax.dot_general(rows_acts, gate_w, contract_last, preferred_element_type=jnp.float32)
    pre_up = lax.dot_general(rows_acts, up_w, contract_last, preferred_element_type=jnp.float32)
    sigma = jax.nn.sigmoid(pre_gate)
    swish = pre_gate * sigma
    hidden = (swish * pre_up).astype(jnp.bfloat16)
    expert_out = jnp.dot(hidden, down_w, preferred_element_type=jnp.float32)
    gate_part = jnp.sum(expert_out * rows_grad.astype(jnp.float32), axis=1)
    scaled_grad = (rows_gate.astype(jnp.float32)[:, None] * rows_grad.astype(jnp.float32)).astype(
        jnp.bfloat16
    )
    hidden_grad = lax.dot_general(
        scaled_grad, down_w, contract_last, preferred_element_type=jnp.float32
    )
    grad_gate_pre = (hidden_grad * pre_up * sigma * (1.0 + pre_gate * (1.0 - sigma))).astype(
        jnp.bfloat16
    )
    grad_up_pre = (hidden_grad * swish).astype(jnp.bfloat16)
    down_grad = lax.dot_general(
        hidden, scaled_grad, contract_first, preferred_element_type=jnp.float32
    ).astype(jnp.bfloat16)
    gate_grad = lax.dot_general(
        grad_gate_pre, rows_acts, contract_first, preferred_element_type=jnp.float32
    ).astype(jnp.bfloat16)
    up_grad = lax.dot_general(
        grad_up_pre, rows_acts, contract_first, preferred_element_type=jnp.float32
    ).astype(jnp.bfloat16)
    row_terms = jnp.dot(grad_gate_pre, gate_w, preferred_element_type=jnp.float32)
    row_terms = row_terms + jnp.dot(grad_up_pre, up_w, preferred_element_type=jnp.float32)
    row_share = lax.psum_scatter(
        row_terms.astype(jnp.bfloat16), "rep", scatter_dimension=1, tiled=True
    )
    gate_total = lax.psum(gate_part, "rep").astype(jnp.bfloat16)
    back_share, back_gate = (
        lax.all_to_all(row_share, ("ctx", "exp"), split_axis=0, concat_axis=0, tiled=True),
        lax.all_to_all(gate_total, ("ctx", "exp"), split_axis=0, concat_axis=0, tiled=True),
    )
    acts_grad = lax.dot_general(
        placing, back_share, contract_first, preferred_element_type=jnp.float32
    ).astype(jnp.bfloat16)
    gate_flat = lax.dot_general(
        select, back_gate, contract_first, preferred_element_type=jnp.float32
    )
    gate_grad_tok = gate_flat.reshape(tokens_here, top_count).astype(jnp.bfloat16)
    return (acts_grad, gate_grad_tok, gate_grad[None], up_grad[None], down_grad[None])


def solution(mesh):
    placed = (
        P(("ctx", "exp"), "rep"),
        P(("ctx", "exp"), "rep"),
        P(("ctx", "exp"), None),
        P(("ctx", "exp"), None),
        P(("ctx", "exp"), "rep", None),
        P(("ctx", "exp"), "rep", None),
        P(("ctx", "exp"), "rep", None),
    )
    return jax.shard_map(
        body,
        mesh=mesh,
        in_specs=placed,
        out_specs=(
            P(("ctx", "exp"), "rep"),
            P(("ctx", "exp"), None),
            P(("ctx", "exp"), "rep", None),
            P(("ctx", "exp"), "rep", None),
            P(("ctx", "exp"), "rep", None),
        ),
        check_vma=False,
    )
```

profile of v0, /device:TPU:1, one launch (start us, length us, event | category | flops | bytes accessed | tf_op | source)
XLA Modules:
  0.0 281.5 jit_solution(562904140357769885)
XLA Ops:
  7.2 0.8 copy.24
  8.2 0.8 copy.28
  9.2 0.2 fusion.22
  9.7 0.2 convolution_reduce_fusion
  9.9 0.9 all_to_all.49
  10.8 20.8 %all-to-all-start = ((bf16[128,3,1]{1,2,0:T(2,128)(2,1)}), bf16[128,3,1]{1,2,0:T(2,128)(2,1)S(1)}, u32[]{:S(2)}, u32[]{:S(2)}) async-start(bf16[128,3,1]{1,2,0:T(2,128)(2,1)} %all_to_all.49), calls=%async_computation | async-start | bytes 131072 | tf_op jit(solution)/shard_map/all_to_all | solution.py:37
  31.7 0.2 fusion.19
  31.9 6.4 %all_gather.6 = bf16[32,2048]{1,0:T(8,128)(2,1)S(1)} all-gather(bf16[32,512]{1,0:T(8,128)(2,1)} %param.8), channel_id=1, replica_groups=mesh['ctx'=8,'exp'=16,'rep'=4] {'rep'}, dimensions={1}, use_global_device_ids=true | all-gather | bytes 163840 | tf_op jit(solution)/shard_map/all_gather | solution.py:30
  38.3 0.6 convolution_convert_fusion.1
  38.9 2.3 all_to_all.38
  41.3 3.4 %all-to-all-done = bf16[128,3,1]{1,2,0:T(2,128)(2,1)S(1)} async-done(((bf16[128,3,1]{1,2,0:T(2,128)(2,1)}), bf16[128,3,1]{1,2,0:T(2,128)(2,1)S(1)}, u32[]{:S(2)}, u32[]{:S(2)}) %all-to-all-start) | async-done | bytes 800 | tf_op jit(solution)/shard_map/all_to_all | solution.py:37
  44.7 12.6 %all-to-all-start.1 = ((bf16[128,3,2048]{2,1,0:T(4,128)(2,1)}), bf16[128,3,2048]{2,1,0:T(4,128)(2,1)S(1)}, u32[]{:S(2)}, u32[]{:S(2)}) async-start(bf16[128,3,2048]{2,1,0:T(4,128)(2,1)} %all_to_all.38), calls=%async_computation.1 | async-start | bytes 4194304 | tf_op jit(solution)/shard_map/all_to_all | solution.py:36
  57.3 47.2 %all_gather.7 = bf16[32,2048]{1,0:T(8,128)(2,1)S(1)} all-gather(bf16[32,512]{1,0:T(8,128)(2,1)S(1)} %copy-done.8), channel_id=1, replica_groups=mesh['ctx'=8,'exp'=16,'rep'=4] {'rep'}, dimensions={1}, use_global_device_ids=true | all-gather | bytes 163840 | tf_op jit(solution)/shard_map/all_gather | solution.py:29
  104.5 1.8 convolution_convert_fusion
  106.3 5.2 %all_to_all.40 = bf16[128,3,2048]{2,1,0:T(4,128)(2,1)} reshape(bf16[384,2048]{1,0:T(8,128)(2,1)} %convolution_convert_fusion) | data formatting | bytes 3145728 | tf_op jit(solution)/shard_map/all_to_all | solution.py:35
  111.5 7.1 %all-to-all-done.1 = bf16[128,3,2048]{2,1,0:T(4,128)(2,1)S(1)} async-done(((bf16[128,3,2048]{2,1,0:T(4,128)(2,1)}), bf16[128,3,2048]{2,1,0:T(4,128)(2,1)S(1)}, u32[]{:S(2)}, u32[]{:S(2)}) %all-to-all-start.1) | async-done | bytes 1572896 | tf_op jit(solution)/shard_map/all_to_all | solution.py:36
  118.6 19.2 %all-to-all-start.2 = ((bf16[128,3,2048]{2,1,0:T(4,128)(2,1)}), bf16[128,3,2048]{2,1,0:T(4,128)(2,1)}, u32[]{:S(2)}, u32[]{:S(2)}) async-start(bf16[128,3,2048]{2,1,0:T(4,128)(2,1)} %all_to_all.40), calls=%async_computation.2 | async-start | bytes 4194304 | tf_op jit(solution)/shard_map/all_to_all | solution.py:35
  137.7 0.2 reduce-scatter.2.cloned.1.call-start
  138.0 2.3 multiply_convert_fusion
  140.3 5.0 %convert_element_type.96 = bf16[384,2048]{1,0:T(8,128)(2,1)} reshape(bf16[128,3,2048]{2,1,0:T(4,128)(2,1)} %multiply_convert_fusion) | data formatting | bytes 3145728 | tf_op jit(solution)/shard_map/convert_element_type | solution.py:51
  145.4 46.0 %all-to-all-done.2 = bf16[128,3,2048]{2,1,0:T(4,128)(2,1)} async-done(((bf16[128,3,2048]{2,1,0:T(4,128)(2,1)}), bf16[128,3,2048]{2,1,0:T(4,128)(2,1)}, u32[]{:S(2)}, u32[]{:S(2)}) %all-to-all-start.2) | async-done | bytes 1572896 | tf_op jit(solution)/shard_map/all_to_all | solution.py:35
  191.4 3.9 %all_to_all.42 = bf16[384,2048]{1,0:T(8,128)(2,1)S(1)} reshape(bf16[128,3,2048]{2,1,0:T(4,128)(2,1)} %all-to-all-done.2) | data formatting | bytes 3145728 | tf_op jit(solution)/shard_map/all_to_all | solution.py:35
  195.3 2.0 fusion.6
  197.3 0.7 fusion.12
  198.0 0.7 multiply_convert_fusion.3
  198.8 0.4 copy-done.5
  199.1 0.6 fusion.4
  199.7 1.8 add_convert_fusion
  201.5 5.3 %reshape.95 = f32[384,2048]{1,0:T(8,128)} reshape(bf16[128,3,2048]{2,1,0:T(4,128)(2,1)} %copy-done.2) | data formatting | bytes 4718592 | tf_op jit(solution)/shard_map/convert_element_type | solution.py:51
  206.8 2.6 multiply_reduce_fusion
  209.4 8.1 %psum.7 = bf16[384]{0:T(512)(128)(2,1)S(1)} all-reduce(f32[384]{0:T(512)S(1)} %multiply_reduce_fusion), channel_id=1, replica_groups=mesh['ctx'=8,'exp'=16,'rep'=4] {'rep'}, use_global_device_ids=true, to_apply=%region_6.7 | all-reduce | flops 384 | bytes 2304 | tf_op jit(solution)/shard_map/psum | solution.py:75
  217.5 0.9 all_to_all.50
  218.4 15.2 %all-to-all-start.4 = ((bf16[128,3,1]{1,2,0:T(2,128)(2,1)}), bf16[128,3,1]{1,2,0:T(2,128)(2,1)S(1)}, u32[]{:S(2)}, u32[]{:S(2)}) async-start(bf16[128,3,1]{1,2,0:T(2,128)(2,1)} %all_to_all.50), calls=%async_computation.5 | async-start | bytes 131072 | tf_op jit(solution)/shard_map/all_to_all | solution.py:78
  233.6 0.2 convert_reduce_fusion
  233.8 0.2 reshape.96
  234.0 2.1 all_to_all.43
  236.1 10.6 %all-to-all-done.4 = bf16[128,3,1]{1,2,0:T(2,128)(2,1)S(1)} async-done(((bf16[128,3,1]{1,2,0:T(2,128)(2,1)}), bf16[128,3,1]{1,2,0:T(2,128)(2,1)S(1)}, u32[]{:S(2)}, u32[]{:S(2)}) %all-to-all-start.4) | async-done | bytes 800 | tf_op jit(solution)/shard_map/all_to_all | solution.py:78
  246.7 6.4 %all-to-all-start.3 = ((bf16[128,3,512]{2,1,0:T(4,128)(2,1)}), bf16[128,3,512]{2,1,0:T(4,128)(2,1)S(1)}, u32[]{:S(2)}, u32[]{:S(2)}) async-start(bf16[128,3,512]{2,1,0:T(4,128)(2,1)} %all_to_all.43), calls=%async_computation.4 | async-start | bytes 1048576 | tf_op jit(solution)/shard_map/all_to_all | solution.py:77
  253.1 1.5 fusion
  254.5 1.5 fusion.1
  256.0 1.5 fusion.2
  257.5 0.2 reduce.2
  257.7 0.2 reshape.99
  257.9 0.8 fusion.16
  258.7 0.7 copy.31
  259.4 14.2 %all-to-all-done.3 = bf16[128,3,512]{2,1,0:T(4,128)(2,1)S(1)} async-done(((bf16[128,3,512]{2,1,0:T(4,128)(2,1)}), bf16[128,3,512]{2,1,0:T(4,128)(2,1)S(1)}, u32[]{:S(2)}, u32[]{:S(2)}) %all-to-all-start.3) | async-done | bytes 393248 | tf_op jit(solution)/shard_map/all_to_all | solution.py:77
  273.5 0.3 all_to_all.45
  273.9 0.8 convolution_convert_fusion.5
  (33 shorter events, 0.9 us)
Async XLA Ops:
  7.2 190.8 %copy-start = (bf16[1,192,2048]{2,1,0:T(8,128)(2,1)S(1)}, bf16[1,192,2048]{2,1,0:T(8,128)(2,1)}, u32[]{:S(2)}) copy-start(bf16[1,192,2048]{2,1,0:T(8,128)(2,1)} %param.12) | copy-start | bytes 2359300
  10.8 33.9 %all-to-all-start = ((bf16[128,3,1]{1,2,0:T(2,128)(2,1)}), bf16[128,3,1]{1,2,0:T(2,128)(2,1)S(1)}, u32[]{:S(2)}, u32[]{:S(2)}) async-start(bf16[128,3,1]{1,2,0:T(2,128)(2,1)} %all_to_all.49), calls=%async_computation | async-start | bytes 131072 | tf_op jit(solution)/shard_map/all_to_all | solution.py:37
  41.3 16.0 %copy-start.8 = (bf16[32,512]{1,0:T(8,128)(2,1)S(1)}, bf16[32,512]{1,0:T(8,128)(2,1)}, u32[]{:S(2)}) copy-start(bf16[32,512]{1,0:T(8,128)(2,1)} %param.7) | copy-start | bytes 98308
  44.7 73.9 %all-to-all-start.1 = ((bf16[128,3,2048]{2,1,0:T(4,128)(2,1)}), bf16[128,3,2048]{2,1,0:T(4,128)(2,1)S(1)}, u32[]{:S(2)}, u32[]{:S(2)}) async-start(bf16[128,3,2048]{2,1,0:T(4,128)(2,1)} %all_to_all.38), calls=%async_computation.1 | async-start | bytes 4194304 | tf_op jit(solution)/shard_map/all_to_all | solution.py:36
  118.6 19.5 %copy-start.2 = (bf16[128,3,2048]{2,1,0:T(4,128)(2,1)}, bf16[128,3,2048]{2,1,0:T(4,128)(2,1)S(1)}, u32[]{:S(2)}) copy-start(bf16[128,3,2048]{2,1,0:T(4,128)(2,1)S(1)} %all-to-all-done.1) | copy-start | bytes 4718596
  118.6 72.8 %all-to-all-start.2 = ((bf16[128,3,2048]{2,1,0:T(4,128)(2,1)}), bf16[128,3,2048]{2,1,0:T(4,128)(2,1)}, u32[]{:S(2)}, u32[]{:S(2)}) async-start(bf16[128,3,2048]{2,1,0:T(4,128)(2,1)} %all_to_all.40), calls=%async_computation.2 | async-start | bytes 4194304 | tf_op jit(solution)/shard_map/all_to_all | solution.py:35
  137.7 96.3 %reduce-scatter.2.cloned.1.call-start = ((), (), s32[]{:S(2)}) async-start(), calls=%async_computation.6 | async-start | bytes 1966080 | tf_op jit(solution)/shard_map/reduce_scatter | solution.py:72
  195.3 2.0 copy-start.3
  195.3 2.0 copy-start.4
  198.0 1.1 copy-start.5
  198.7 1.0 copy-start.6
  209.4 43.7 %copy-start.7 = (bf16[384,192]{0,1:T(8,128)(2,1)S(1)}, bf16[384,192]{0,1:T(8,128)(2,1)}, u32[]{:S(2)}) copy-start(bf16[384,192]{0,1:T(8,128)(2,1)} %copy-done.6) | copy-start | bytes 442372
  218.4 28.3 %all-to-all-start.4 = ((bf16[128,3,1]{1,2,0:T(2,128)(2,1)}), bf16[128,3,1]{1,2,0:T(2,128)(2,1)S(1)}, u32[]{:S(2)}, u32[]{:S(2)}) async-start(bf16[128,3,1]{1,2,0:T(2,128)(2,1)} %all_to_all.50), calls=%async_computation.5 | async-start | bytes 131072 | tf_op jit(solution)/shard_map/all_to_all | solution.py:78
  246.7 26.9 %all-to-all-start.3 = ((bf16[128,3,512]{2,1,0:T(4,128)(2,1)}), bf16[128,3,512]{2,1,0:T(4,128)(2,1)S(1)}, u32[]{:S(2)}, u32[]{:S(2)}) async-start(bf16[128,3,512]{2,1,0:T(4,128)(2,1)} %all_to_all.43), calls=%async_computation.4 | async-start | bytes 1048576 | tf_op jit(solution)/shard_map/all_to_all | solution.py:77
  253.1 2.9 %copy-start.1 = (f32[384,2048]{1,0:T(8,128)S(1)}, f32[384,2048]{1,0:T(8,128)}, u32[]{:S(2)}) copy-start(f32[384,2048]{1,0:T(8,128)} %reshape.95) | copy-start | bytes 9437188
Sparse Core Ops, SparseCore 0:
  201.7 31.6 reduce-scatter.1
where the time goes:
time: 283 us; the launch traced here: 282 us
  waiting for transfers between devices  81.3 us (29%)
  starting transfers between devices  74.4 us (26%)
  blocking collectives  61.8 us (22%)
  local copies, waits for them, and re-layouts  29.6 us (10%)
  matrix products  16.8 us (6%)
  between operations  14.3 us (5%)
  other arithmetic  3.36 us (1%)
    all_gather x1, blocking collectives, body(): lax.all_gather(acts, 'rep', axis=1, tiled=True)  47.2 us
    all_to_all x1, waiting for transfers between devices, body(): lax.all_to_all(send_acts, ('ctx', 'exp'), split_axis=0, concat_axis=0, ti...  46 us
    all_to_all x1, starting transfers between devices, body(): lax.all_to_all(slot_gate, ('ctx', 'exp'), split_axis=0, concat_axis=0, ti...  20.8 us
    all_to_all x1, starting transfers between devices, body(): lax.all_to_all(send_acts, ('ctx', 'exp'), split_axis=0, concat_axis=0, ti...  19.2 us
    all_to_all x1, starting transfers between devices, body(): lax.all_to_all(gate_total, ('ctx', 'exp'), split_axis=0, concat_axis=0, t...  15.2 us
    all_to_all x1, waiting for transfers between devices, body(): lax.all_to_all(row_share, ('ctx', 'exp'), split_axis=0, concat_axis=0, ti...  14.2 us
    all_to_all x1, starting transfers between devices, body(): lax.all_to_all(send_grad, ('ctx', 'exp'), split_axis=0, concat_axis=0, ti...  12.6 us
    all_to_all x1, waiting for transfers between devices, body(): lax.all_to_all(gate_total, ('ctx', 'exp'), split_axis=0, concat_axis=0, t...  10.6 us
  transfers between devices with their start and end apart: 6, of which 5 were waited for; matrix products, arithmetic and copies ran while one was open for 9% of the time, Pallas kernels for 0%

commit v1 on v0

v1 whole, which is shorter than its diff:
```python
import jax
import jax.numpy as jnp
from jax import lax
from jax.experimental import pallas as pl
from jax.experimental.pallas import tpu as pltpu
from jax.sharding import PartitionSpec as P

BF16 = jnp.bfloat16
F32 = jnp.float32
LANES = 128
GROUP = ("ctx", "exp")
LAST = (((1,), (1,)), ((), ()))
FIRST = (((0,), (0,)), ((), ()))


def swap(x, bit):
    return lax.ppermute(x, "rep", [(i, i ^ bit) for i in range(lax.axis_size("rep"))])


def expert_kernel(me_ref, own_ref, core_ref, chip_ref, far_ref, wg_ref, wu_ref, wd_ref,
                  keep_ref, send_ref, hid_ref, ggp_ref, gup_ref):
    rows, both = own_ref.shape
    width = both // 2
    me = me_ref[0]
    pre_gate = pre_up = hid_grad = None
    shares = []
    for j, x_ref in enumerate((own_ref, core_ref, chip_ref, far_ref)):
        share = pl.ds(pl.multiple_of((me ^ j) * width, width), width)
        shares.append(share)
        acts = x_ref[:, :width]
        grad = x_ref[:, width:]
        a = lax.dot_general(acts, wg_ref[:, share], LAST, preferred_element_type=F32)
        b = lax.dot_general(acts, wu_ref[:, share], LAST, preferred_element_type=F32)
        c = lax.dot_general(grad, wd_ref[:, share], LAST, preferred_element_type=F32)
        pre_gate = a if j == 0 else pre_gate + a
        pre_up = b if j == 0 else pre_up + b
        hid_grad = c if j == 0 else hid_grad + c
    sigma = jax.nn.sigmoid(pre_gate)
    swish = pre_gate * sigma
    hidden = (swish * pre_up).astype(BF16)
    ggp = (hid_grad * pre_up * sigma * (1.0 + pre_gate * (1.0 - sigma))).astype(BF16)
    gup = (hid_grad * swish).astype(BF16)
    hid_ref[...] = hidden
    ggp_ref[...] = ggp
    gup_ref[...] = gup
    gate = jnp.sum(hidden.astype(F32) * hid_grad, axis=1, keepdims=True)
    count = rows // 3
    lane = lax.broadcasted_iota(jnp.int32, (count, LANES), 1)
    table = jnp.zeros((count, LANES), F32)
    for c in range(3):
        table = jnp.where(lane == c, gate[c * count:(c + 1) * count], table)
    table = table.astype(BF16)
    high = count * LANES // width
    for j, out_ref in enumerate((keep_ref, send_ref, keep_ref, send_ref)):
        terms = jnp.dot(ggp, wg_ref[:, shares[j]], preferred_element_type=F32)
        terms = terms + jnp.dot(gup, wu_ref[:, shares[j]], preferred_element_type=F32)
        out_ref[j // 2, :rows, :] = terms.astype(BF16)
        for q in range(width // LANES):
            out_ref[j // 2, rows:, q * LANES:(q + 1) * LANES] = table[q * high:(q + 1) * high]


def weight_kernel(me_ref, own_ref, core_ref, chip_ref, far_ref, hid_ref, ggp_ref, gup_ref,
                  wg_out, wu_out, wd_out):
    width = own_ref.shape[1] // 2
    me = me_ref[0]
    hid, ggp, gup = hid_ref[...].T, ggp_ref[...].T, gup_ref[...].T
    for j, x_ref in enumerate((own_ref, core_ref, chip_ref, far_ref)):
        share = pl.ds(pl.multiple_of((me ^ j) * width, width), width)
        acts = x_ref[:, :width]
        grad = x_ref[:, width:]
        wg_out[:, share] = jnp.dot(ggp, acts, preferred_element_type=F32).astype(BF16)
        wu_out[:, share] = jnp.dot(gup, acts, preferred_element_type=F32).astype(BF16)
        wd_out[:, share] = jnp.dot(hid, grad, preferred_element_type=F32).astype(BF16)


def call(kernel, outs, flops, moved, *args):
    vmem = pl.BlockSpec(memory_space=pltpu.VMEM)
    smem = pl.BlockSpec(memory_space=pltpu.SMEM)
    return pl.pallas_call(
        kernel,
        out_shape=[jax.ShapeDtypeStruct(s, BF16) for s in outs],
        in_specs=[smem] + [vmem] * (len(args) - 1),
        out_specs=[vmem] * len(outs),
        cost_estimate=pl.CostEstimate(flops=flops, bytes_accessed=moved, transcendentals=0),
        compiler_params=pltpu.CompilerParams(vmem_limit_bytes=40 << 20),
    )(*args)


def body(acts, grad_out, experts_idx, gate_prob, w_gate, w_up, w_down):
    tokens, top = experts_idx.shape
    width = acts.shape[1]
    experts = lax.axis_size(GROUP)
    cap = 3
    rows = cap * experts
    units, features = w_gate.shape[1:]
    me = lax.axis_index("rep").astype(jnp.int32).reshape(1)

    label = jnp.arange(experts, dtype=jnp.int32)
    hit = experts_idx.T[None, :, :] == label[:, None, None]
    named = jnp.any(hit, axis=1)
    earlier = jnp.arange(tokens)[:, None] < jnp.arange(tokens)[None, :]
    rank = jnp.dot(named.astype(BF16), earlier.astype(BF16), preferred_element_type=F32)
    gate_of = jnp.sum(jnp.where(hit, gate_prob.T[None].astype(F32), 0.0), axis=1)
    slot = jnp.where(named, rank, -1.0)
    placed = slot[:, None, :] == jnp.arange(cap, dtype=F32)[None, :, None]
    placing = placed.astype(BF16).reshape(rows, tokens)
    scaling = jnp.where(placed, gate_of[:, None, :], 0.0).astype(BF16).reshape(rows, tokens)
    send = jnp.concatenate(
        [
            jnp.dot(placing, acts, preferred_element_type=F32).astype(BF16),
            jnp.dot(scaling, grad_out, preferred_element_type=F32).astype(BF16),
        ],
        axis=1,
    ).reshape(experts, cap * 2 * width // LANES, LANES)
    got = lax.all_to_all(send, GROUP, split_axis=0, concat_axis=0, tiled=True)
    own = got.reshape(experts, cap, 2 * width).transpose(1, 0, 2).reshape(rows, 2 * width)
    chip = swap(own, 2)
    core = swap(own, 1)
    far = swap(chip, 1)
    pieces = (me, own, core, chip, far)

    wide = rows + experts * LANES // width
    product = 2 * rows * units * features
    keep, away, hid, ggp, gup = call(
        expert_kernel,
        [(2, wide, width)] * 2 + [(rows, units)] * 3,
        5 * product,
        (3 * units + 3 * rows) * features * 2,
        *pieces, w_gate[0], w_up[0], w_down[0],
    )
    near = keep + swap(away, 1)
    total = near[0] + swap(near[1], 2)
    wg_grad, wu_grad, wd_grad = call(
        weight_kernel, [(units, features)] * 3, 3 * product, (3 * units + 2 * rows) * features * 2,
        *pieces, hid, ggp, gup,
    )
    table = jnp.concatenate(
        [total[rows:, q * LANES:(q + 1) * LANES] for q in range(width // LANES)], axis=0
    )
    table = jnp.pad(table, ((0, 0), (0, width - LANES)))
    back = jnp.concatenate([total[:rows].reshape(cap, experts, width), table[None]], axis=0)
    back = lax.all_to_all(back.transpose(1, 0, 2), GROUP, split_axis=0, concat_axis=0, tiled=True)

    acts_grad = lax.dot_general(
        placing, back[:, :cap].reshape(rows, width), FIRST, preferred_element_type=F32
    ).astype(BF16)
    flat = experts_idx.reshape(-1)
    picked = (flat[:, None] == label[None, :]).astype(BF16)
    lines = jnp.dot(picked, back[:, cap, :LANES], preferred_element_type=F32)
    mine = jnp.sum(
        jnp.where(hit, rank[:, None, :], 0.0), axis=0
    ).T.reshape(-1)
    lane = jnp.arange(LANES, dtype=F32)
    gates = jnp.sum(jnp.where(lane[None, :] == mine[:, None], lines, 0.0), axis=1)
    gate_grad = (gates.reshape(tokens, top) / gate_prob.astype(F32)).astype(BF16)
    return (acts_grad, gate_grad, wg_grad[None], wu_grad[None], wd_grad[None])


def solution(mesh):
    rows = P(GROUP, "rep")
    table = P(GROUP, None)
    weight = P(GROUP, "rep", None)
    return jax.shard_map(
        body,
        mesh=mesh,
        in_specs=(rows, rows, table, table, weight, weight, weight),
        out_specs=(rows, table, weight, weight, weight),
        check_vma=False,
    )
```

time: 283 us -> 138 us (0.49)
  starting transfers between devices: 74.4 us -> 22.5 us
  waiting for transfers between devices: 81.3 us -> 44.2 us
  local copies, waits for them, and re-layouts: 29.6 us -> 9.95 us
  matrix products: 16.8 us -> 2.82 us
  blocking collectives: 61.8 us -> 48.1 us
  between operations: 14.3 us -> 0.98 us
  Pallas kernels: 0 us -> 5.72 us
    all_to_all x5 -> x1, starting transfers between devices: 74.1 us -> 8.16 us  [body(): lax.all_to_all(back.transpose(1, 0, 2), GROUP, split_axis=0, concat_axis=...]
    all_to_all x5 -> x1, waiting for transfers between devices: 81.3 us -> 15.7 us  [body(): lax.all_to_all(back.transpose(1, 0, 2), GROUP, split_axis=0, concat_axis=...]
    all_gather x2 -> x0, blocking collectives: 53.7 us -> none  [the longest x1 47.2 us: body(): lax.all_gather(acts, 'rep', axis=1, tiled=True)]
    all_to_all x0 -> x1, blocking collectives: none -> 48.1 us  [body(): got = lax.all_to_all(send, GROUP, split_axis=0, concat_axis=0, tiled=True)]
    ppermute x0 -> x5, waiting for transfers between devices: none -> 28.5 us  [swap(): lax.ppermute(x, 'rep', [(i, i ^ bit) for i in range(lax.axis_size('rep'))])]
    all_to_all x8 -> x1, local copies, waits for them, and re-layouts: 15.8 us -> 0.53 us  [body(): got = lax.all_to_all(send, GROUP, split_axis=0, concat_axis=0, tiled=True)]
    ppermute x0 -> x5, starting transfers between devices: none -> 14.3 us  [swap(): lax.ppermute(x, 'rep', [(i, i ^ bit) for i in range(lax.axis_size('rep'))])]
    dot_general x14 -> x5, matrix products: 16.8 us -> 2.82 us  [the longest x1 1.89 us: body(): lax.dot_general(placing, back[:, :cap].reshape(rows, width), FIRST, prefe...]
  transfers between devices with their start and end apart: 6 -> 6, of which waited for: 5 -> 5; matrix products, arithmetic and copies ran while one was open for 9% -> 0% of each run, Pallas kernels for 0% -> 2%
where the time goes in v1:
time: 138 us; the launch traced here: 137 us
  blocking collectives  48.1 us (35%)
  waiting for transfers between devices  44.2 us (32%)
  starting transfers between devices  22.5 us (16%)
  local copies, waits for them, and re-layouts  9.95 us (7%)
  Pallas kernels  5.72 us (4%)
  other arithmetic  2.97 us (2%)
  matrix products  2.82 us (2%)
    all_to_all x1, blocking collectives, body(): got = lax.all_to_all(send, GROUP, split_axis=0, concat_axis=0, tiled=True)  48.1 us
    ppermute x5, waiting for transfers between devices, swap(): lax.ppermute(x, 'rep', [(i, i ^ bit) for i in range(lax.axis_size('rep'))])  28.5 us
    all_to_all x1, waiting for transfers between devices, body(): lax.all_to_all(back.transpose(1, 0, 2), GROUP, split_axis=0, concat_axis=...  15.7 us
    ppermute x5, starting transfers between devices, swap(): lax.ppermute(x, 'rep', [(i, i ^ bit) for i in range(lax.axis_size('rep'))])  14.3 us
    all_to_all x1, starting transfers between devices, body(): lax.all_to_all(back.transpose(1, 0, 2), GROUP, split_axis=0, concat_axis=...  8.16 us
    unnamed x25, local copies, waits for them, and re-layouts  6.11 us
    pallas_call x2, Pallas kernels, call(): pl.pallas_call(kernel, out_shape=[jax.ShapeDtypeStruct(s, BF16) for s in...  5.72 us
  transfers between devices with their start and end apart: 6, of which 5 were waited for; matrix products, arithmetic and copies ran while one was open for 0% of the time, Pallas kernels for 2%

profile of v1, /device:TPU:1, one launch (start us, length us, event | category | flops | bytes accessed | tf_op | source)
XLA Modules:
  0.0 137.3 jit_solution(11435778564202511340)
XLA Ops:
  0.7 0.8 fusion.13
  1.5 0.2 broadcast_select_fusion
  1.7 0.1 copy.47
  1.9 0.1 eq.74
  2.0 0.2 eq.76
  2.2 0.1 copy.48
  2.4 0.2 select_reduce_fusion
  2.6 0.1 copy.50
  2.7 0.1 broadcast_in_dim.71
  2.8 0.1 broadcast_compare_fusion
  3.0 0.2 convolution_convert_fusion.1
  3.2 0.2 convolution_convert_fusion
  3.5 0.1 pad_maximum_fusion
  3.6 0.3 reshape.45
  3.9 48.1 %all_to_all.10 = bf16[128,24,128]{2,1,0:T(8,128)(2,1)S(1)} all-to-all(bf16[128,24,128]{2,1,0:T(8,128)(2,1)S(1)} %reshape.45), channel_id=1, replica_groups=mesh['ctx'=8,'exp'=16,'rep'=4] {'ctx','exp'}, dimensions={0} | all-to-all | bytes 1572864 | tf_op jit(solution)/shard_map/all_to_all | solution.py:115
  52.0 0.5 copy.51
  52.6 0.3 copy.52
  52.9 1.9 %collective-permute-start.1 = (bf16[384,1024]{1,0:T(8,128)(2,1)S(1)}, bf16[384,1024]{1,0:T(8,128)(2,1)S(1)}, u32[]{:S(2)}, u32[]{:S(2)}) collective-permute-start(bf16[384,1024]{1,0:T(8,128)(2,1)S(1)} %bitcast.38), channel_id=1, source_target_pairs={{0,2},{1,3},{2,0},{3,1},{4,6},{5,7},{6,4},{7,5},{8,10},{9,11},{10,... | collective-permute-start | bytes 2359304 | tf_op jit(solution)/shard_map/ppermute | solution.py:17
  54.8 3.7 %collective-permute-start = (bf16[384,1024]{1,0:T(8,128)(2,1)S(1)}, bf16[384,1024]{1,0:T(8,128)(2,1)S(1)}, u32[]{:S(2)}, u32[]{:S(2)}) collective-permute-start(bf16[384,1024]{1,0:T(8,128)(2,1)S(1)} %bitcast.39), channel_id=1, source_target_pairs={{0,1},{1,0},{2,3},{3,2},{4,5},{5,4},{6,7},{7,6},{8,9},{9,8},{10,11... | collective-permute-start | bytes 2359304 | tf_op jit(solution)/shard_map/ppermute | solution.py:17
  58.5 13.6 %collective-permute-done.1.chip_ref = bf16[384,1024]{1,0:T(8,128)(2,1)S(1)} collective-permute-done((bf16[384,1024]{1,0:T(8,128)(2,1)S(1)}, bf16[384,1024]{1,0:T(8,128)(2,1)S(1)}, u32[]{:S(2)}, u32[]{:S(2)}) %collective-permute-start.1) | collective-permute-done | bytes 786464 | tf_op jit(solution)/shard_map/ppermute | solution.py:17
  72.0 4.6 %collective-permute-start.2 = (bf16[384,1024]{1,0:T(8,128)(2,1)S(1)}, bf16[384,1024]{1,0:T(8,128)(2,1)S(1)}, u32[]{:S(2)}, u32[]{:S(2)}) collective-permute-start(bf16[384,1024]{1,0:T(8,128)(2,1)S(1)} %collective-permute-done.1.chip_ref), channel_id=1, source_target_pairs={{0,1},{1,0},{2,3},{3,2},{4,5},{5,4},{6,7},{7,6},{8,9},{9,8},{10,11... | collective-permute-start | bytes 2359304 | tf_op jit(solution)/shard_map/ppermute | solution.py:17
  76.6 1.9 %collective-permute-done.2.far_ref = bf16[384,1024]{1,0:T(8,128)(2,1)S(1)} collective-permute-done((bf16[384,1024]{1,0:T(8,128)(2,1)S(1)}, bf16[384,1024]{1,0:T(8,128)(2,1)S(1)}, u32[]{:S(2)}, u32[]{:S(2)}) %collective-permute-start.2) | collective-permute-done | bytes 786464 | tf_op jit(solution)/shard_map/ppermute | solution.py:17
  78.5 1.1 copy-done.5
  79.6 1.1 copy-done.6
  80.8 1.1 copy-done.7
  81.9 3.1 %shard_map.110 = (bf16[2,416,512]{2,1,0:T(8,128)(2,1)S(1)}, bf16[2,416,512]{2,1,0:T(8,128)(2,1)S(1)}, bf16[384,192]{1,0:T(8,128)(2,1)S(1)}, bf16[384,192]{1,0:T(8,128)(2,1)S(1)}, bf16[384,192]{1,0:T(8,128)(2,1)S(1)}) custom-call(s32[1]{0:T(128)} %bitcast.1.me_ref, bf16[384,1024]{1,0:T(8,128)(2,1)S(1)} %bitcast.40, ...), custom_call_target="tpu_custom_call" | custom-call | flops 1509949440 | bytes 7077888 | tf_op jit(solution)/shard_map/pallas_call | solution.py:79
  85.0 2.3 %collective-permute-start.3 = (bf16[2,416,512]{2,1,0:T(8,128)(2,1)S(1)}, bf16[2,416,512]{2,1,0:T(8,128)(2,1)S(1)}, u32[]{:S(2)}, u32[]{:S(2)}) collective-permute-start(bf16[2,416,512]{2,1,0:T(8,128)(2,1)S(1)} %get-tuple-element.14), channel_id=1, source_target_pairs={{0,1},{1,0},{2,3},{3,2},{4,5},{5,4},{6,7},{7,6},{8,9},{9,8},{10,11... | collective-permute-start | bytes 2555912 | tf_op jit(solution)/shard_map/ppermute | solution.py:17
  87.3 2.0 %collective-permute-done.3 = bf16[2,416,512]{2,1,0:T(8,128)(2,1)S(1)} collective-permute-done((bf16[2,416,512]{2,1,0:T(8,128)(2,1)S(1)}, bf16[2,416,512]{2,1,0:T(8,128)(2,1)S(1)}, u32[]{:S(2)}, u32[]{:S(2)}) %collective-permute-start.3) | collective-permute-done | bytes 852000 | tf_op jit(solution)/shard_map/ppermute | solution.py:17
  89.3 0.2 add.8
  89.6 1.9 %collective-permute-start.4 = (bf16[416,512]{1,0:T(8,128)(2,1)S(1)}, bf16[416,512]{1,0:T(8,128)(2,1)S(1)}, u32[]{:S(2)}, u32[]{:S(2)}) collective-permute-start(bf16[416,512]{1,0:T(8,128)(2,1)S(1)} %slice_bitcast_fusion), channel_id=1, source_target_pairs={{0,2},{1,3},{2,0},{3,1},{4,6},{5,7},{6,4},{7,5},{8,10},{9,11},{10,... | collective-permute-start | bytes 1277960 | tf_op jit(solution)/shard_map/ppermute | solution.py:17
  91.5 11.0 %collective-permute-done.4 = bf16[416,512]{1,0:T(8,128)(2,1)S(1)} collective-permute-done((bf16[416,512]{1,0:T(8,128)(2,1)S(1)}, bf16[416,512]{1,0:T(8,128)(2,1)S(1)}, u32[]{:S(2)}, u32[]{:S(2)}) %collective-permute-start.4) | collective-permute-done | bytes 426016 | tf_op jit(solution)/shard_map/ppermute | solution.py:17
  102.6 0.2 copy.54
  102.9 0.3 copy.53
  103.2 1.3 maximum_bitcast_fusion
  104.5 8.2 %all-to-all-start.1 = ((bf16[128,4,512]{2,1,0:T(4,128)(2,1)}), bf16[128,4,512]{2,1,0:T(4,128)(2,1)}, u32[]{:S(2)}, u32[]{:S(2)}) async-start(bf16[128,4,512]{2,1,0:T(4,128)(2,1)} %maximum_bitcast_fusion), calls=%async_computation.1 | async-start | bytes 1048576 | tf_op jit(solution)/shard_map/all_to_all | solution.py:142
  112.7 0.1 copy.58
  112.8 0.1 eq.83
  112.9 0.1 eq.80
  113.0 0.1 iota_compare_fusion.1
  113.1 0.9 copy-done.2
  114.1 0.9 copy-done.4
  115.0 2.6 %shard_map.111 = (bf16[192,2048]{1,0:T(8,128)(2,1)}, bf16[192,2048]{1,0:T(8,128)(2,1)}, bf16[192,2048]{1,0:T(8,128)(2,1)}) custom-call(s32[1]{0:T(128)} %bitcast.1.me_ref, bf16[384,1024]{1,0:T(8,128)(2,1)S(1)} %bitcast.41, bf16[384,1024]{1,0:T(8,128)(2,1)S(1)} %collective-permute-done.core_ref, bf16[384,1024]{1,0:T(8,128)(2,1)S(1)} %collective-permute-done.1.chip_ref, ...), custom_call_target="tpu_custom_call" | custom-call | flops 905969664 | bytes 5505024 | tf_op jit(solution)/shard_map/pallas_call | solution.py:79
  117.6 15.7 %all-to-all-done.1 = bf16[128,4,512]{2,1,0:T(4,128)(2,1)} async-done(((bf16[128,4,512]{2,1,0:T(4,128)(2,1)}), bf16[128,4,512]{2,1,0:T(4,128)(2,1)}, u32[]{:S(2)}, u32[]{:S(2)}) %all-to-all-start.1) | async-done | bytes 524320 | tf_op jit(solution)/shard_map/all_to_all | solution.py:142
  133.3 1.0 slice.44
  134.3 0.3 fusion
  134.6 0.1 reshape.49
  134.7 0.7 copy.60
  135.4 1.9 %fusion.1 = bf16[32,512]{1,0:T(8,128)(2,1)} fusion(bf16[128,3,512]{2,1,0:T(4,128)(2,1)} %bitcast.37, pred[128,3,32]{2,1,0:T(4,128)(4,1)S(1)} %iota_compare_fusion.1), kind=kOutput, calls=%fused_computation.5 | convolution fusion | flops 12599296 | bytes 438272 | tf_op jit(solution)/shard_map/dot_general | solution.py:144
  (30 shorter events, 0.4 us)
Async XLA Ops:
  0.6 2.3 %copy-start = (bf16[32,512]{1,0:T(8,128)(2,1)S(1)}, bf16[32,512]{1,0:T(8,128)(2,1)}, u32[]{:S(2)}) copy-start(bf16[32,512]{1,0:T(8,128)(2,1)} %param.7) | copy-start | bytes 98308
  0.6 1.7 %copy-start.8 = (s32[32,8]{0,1:T(8,128)S(1)}, s32[32,8]{0,1:T(8,128)}, u32[]{:S(2)}) copy-start(s32[32,8]{0,1:T(8,128)} %param.9) | copy-start | bytes 3076
  0.7 1.5 %copy-start.10 = (bf16[32,8]{0,1:T(8,128)(2,1)S(1)}, bf16[32,8]{0,1:T(8,128)(2,1)}, u32[]{:S(2)}) copy-start(bf16[32,8]{0,1:T(8,128)(2,1)} %param.10) | copy-start | bytes 1540
  1.9 1.3 copy-start.9
  52.9 19.2 %collective-permute-start.1 = (bf16[384,1024]{1,0:T(8,128)(2,1)S(1)}, bf16[384,1024]{1,0:T(8,128)(2,1)S(1)}, u32[]{:S(2)}, u32[]{:S(2)}) collective-permute-start(bf16[384,1024]{1,0:T(8,128)(2,1)S(1)} %bitcast.38), channel_id=1, source_target_pairs={{0,2},{1,3},{2,0},{3,1},{4,6},{5,7},{6,4},{7,5},{8,10},{9,11},{10,... | collective-permute-start | bytes 2359304 | tf_op jit(solution)/shard_map/ppermute | solution.py:17
  54.8 21.8 %collective-permute-start = (bf16[384,1024]{1,0:T(8,128)(2,1)S(1)}, bf16[384,1024]{1,0:T(8,128)(2,1)S(1)}, u32[]{:S(2)}, u32[]{:S(2)}) collective-permute-start(bf16[384,1024]{1,0:T(8,128)(2,1)S(1)} %bitcast.39), channel_id=1, source_target_pairs={{0,1},{1,0},{2,3},{3,2},{4,5},{5,4},{6,7},{7,6},{8,9},{9,8},{10,11... | collective-permute-start | bytes 2359304 | tf_op jit(solution)/shard_map/ppermute | solution.py:17
  72.0 6.5 %collective-permute-start.2 = (bf16[384,1024]{1,0:T(8,128)(2,1)S(1)}, bf16[384,1024]{1,0:T(8,128)(2,1)S(1)}, u32[]{:S(2)}, u32[]{:S(2)}) collective-permute-start(bf16[384,1024]{1,0:T(8,128)(2,1)S(1)} %collective-permute-done.1.chip_ref), channel_id=1, source_target_pairs={{0,1},{1,0},{2,3},{3,2},{4,5},{5,4},{6,7},{7,6},{8,9},{9,8},{10,11... | collective-permute-start | bytes 2359304 | tf_op jit(solution)/shard_map/ppermute | solution.py:17
  78.5 1.1 copy-start.5
  79.6 1.1 copy-start.6
  80.8 1.1 copy-start.7
  85.0 4.5 %copy-start.1 = (bf16[384,192]{1,0:T(8,128)(2,1)}, bf16[384,192]{1,0:T(8,128)(2,1)S(1)}, u32[]{:S(2)}) copy-start(bf16[384,192]{1,0:T(8,128)(2,1)S(1)} %get-tuple-element.16.ggp_ref) | copy-start | bytes 442372
  85.0 4.5 %copy-start.3 = (bf16[384,192]{1,0:T(8,128)(2,1)}, bf16[384,192]{1,0:T(8,128)(2,1)S(1)}, u32[]{:S(2)}) copy-start(bf16[384,192]{1,0:T(8,128)(2,1)S(1)} %get-tuple-element.17.gup_ref) | copy-start | bytes 442372
  85.0 4.3 %collective-permute-start.3 = (bf16[2,416,512]{2,1,0:T(8,128)(2,1)S(1)}, bf16[2,416,512]{2,1,0:T(8,128)(2,1)S(1)}, u32[]{:S(2)}, u32[]{:S(2)}) collective-permute-start(bf16[2,416,512]{2,1,0:T(8,128)(2,1)S(1)} %get-tuple-element.14), channel_id=1, source_target_pairs={{0,1},{1,0},{2,3},{3,2},{4,5},{5,4},{6,7},{7,6},{8,9},{9,8},{10,11... | collective-permute-start | bytes 2555912 | tf_op jit(solution)/shard_map/ppermute | solution.py:17
  89.6 12.9 %collective-permute-start.4 = (bf16[416,512]{1,0:T(8,128)(2,1)S(1)}, bf16[416,512]{1,0:T(8,128)(2,1)S(1)}, u32[]{:S(2)}, u32[]{:S(2)}) collective-permute-start(bf16[416,512]{1,0:T(8,128)(2,1)S(1)} %slice_bitcast_fusion), channel_id=1, source_target_pairs={{0,2},{1,3},{2,0},{3,1},{4,6},{5,7},{6,4},{7,5},{8,10},{9,11},{10,... | collective-permute-start | bytes 1277960 | tf_op jit(solution)/shard_map/ppermute | solution.py:17
  104.5 28.8 %all-to-all-start.1 = ((bf16[128,4,512]{2,1,0:T(4,128)(2,1)}), bf16[128,4,512]{2,1,0:T(4,128)(2,1)}, u32[]{:S(2)}, u32[]{:S(2)}) async-start(bf16[128,4,512]{2,1,0:T(4,128)(2,1)} %maximum_bitcast_fusion), calls=%async_computation.1 | async-start | bytes 1048576 | tf_op jit(solution)/shard_map/all_to_all | solution.py:142
  113.1 0.9 copy-start.2
  114.1 0.9 copy-start.4

commit v2 on v1

v2 whole, which is shorter than its diff:
```python
import jax
import jax.numpy as jnp
from jax import lax
from jax.experimental import pallas as pl
from jax.experimental.pallas import tpu as pltpu
from jax.sharding import PartitionSpec as P

BF16 = jnp.bfloat16
F32 = jnp.float32
LANES = 128
CAP = 3
BLOCK = 16
GROUP = ("ctx", "exp")
LAST = (((1,), (1,)), ((), ()))
FIRST = (((0,), (0,)), ((), ()))


def swap(x, bit):
    return lax.ppermute(x, "rep", [(i, i ^ bit) for i in range(lax.axis_size("rep"))])


def iota(shape, dim):
    return lax.broadcasted_iota(jnp.int32, shape, dim)


def low(x, size):
    return x & (size - 1)


def high(x, size):
    return x >> (size.bit_length() - 1)


def routes(idx, gate, experts, copies):
    top, tokens = idx.shape
    lanes = copies * tokens
    repeat = (low(iota((tokens, lanes), 1), tokens) == iota((tokens, lanes), 0)).astype(F32)
    idx = jnp.dot(idx.astype(F32), repeat, preferred_element_type=F32).astype(jnp.int32)
    gate = jnp.dot(gate.astype(F32), repeat, preferred_element_type=F32)
    label = iota((experts, lanes), 0)
    hits = [idx[k:k + 1] == label for k in range(top)]
    named = jnp.zeros((experts, lanes), F32)
    weight = jnp.zeros((experts, lanes), F32)
    for k in range(top):
        named = jnp.where(hits[k], 1.0, named)
        weight = jnp.where(hits[k], gate[k:k + 1], weight)
    before = iota((lanes, lanes), 0) < low(iota((lanes, lanes), 1), tokens)
    rank = jnp.dot(named.astype(BF16), before.astype(BF16), preferred_element_type=F32)
    slot = jnp.where(named > 0.0, rank, -1.0)
    return hits, slot, weight


def send_kernel(*refs):
    sources, out_ref, code_ref, value_ref, held, made_ref, sems = refs[:4], refs[4], *refs[5:7], refs[7:11], *refs[11:]
    copies_in = [
        pltpu.make_async_copy(source, kept, sems.at[n]) for n, (source, kept) in enumerate(zip(sources, held))
    ]
    for copy in copies_in:
        copy.start()
    for copy in copies_in:
        copy.wait()
    idx_ref, gate_ref, acts_ref, grad_ref = held
    experts = code_ref.shape[0]
    tokens, width = acts_ref.shape
    chunks = width // LANES
    copies = 2 * chunks
    lanes = copies * tokens
    _, slot, weight = routes(idx_ref[...], gate_ref[...], experts, copies)
    chunk = high(iota((experts, lanes), 1), tokens)
    code_ref[...] = jnp.where(slot < 0.0, -1, slot.astype(jnp.int32) * copies + chunk)
    value_ref[...] = jnp.where(chunk < chunks, 1.0, weight)
    parts = [acts_ref[:, q * LANES:(q + 1) * LANES] for q in range(chunks)]
    parts += [grad_ref[:, q * LANES:(q + 1) * LANES] for q in range(chunks)]
    data = jnp.concatenate(parts, axis=0)
    lines = CAP * copies
    size = BLOCK * lines
    line = iota((BLOCK, lines, lanes), 1)
    copies_out = []
    for b in range(experts // BLOCK):
        code = code_ref[b * BLOCK:(b + 1) * BLOCK, :][:, None, :]
        value = value_ref[b * BLOCK:(b + 1) * BLOCK, :][:, None, :]
        place = jnp.where(code == line, value, 0.0).astype(BF16).reshape(size, lanes)
        made_ref[b] = jnp.dot(place, data, preferred_element_type=F32).astype(BF16)
        copies_out.append(
            pltpu.make_async_copy(made_ref.at[b], out_ref.at[b * size:(b + 1) * size, :], sems.at[4 + b])
        )
        copies_out[-1].start()
    for copy in copies_out:
        copy.wait()


def mover():
    lines = CAP * 8
    size = BLOCK * lines
    out, line = iota((size, size), 0), iota((size, size), 1)
    return (low(out, BLOCK) * lines + high(out, BLOCK) == line).astype(BF16)


def unpack(move, raw_ref, out_ref):
    size = move.shape[0]
    chunks = out_ref.shape[1] // LANES
    sources = raw_ref.shape[0] // size * BLOCK
    for b in range(sources // BLOCK):
        made = jnp.dot(move, raw_ref[b * size:(b + 1) * size, :], preferred_element_type=F32).astype(BF16)
        for m in range(size // BLOCK):
            row, lane = m // chunks * sources + b * BLOCK, m % chunks * LANES
            out_ref[row:row + BLOCK, lane:lane + LANES] = made[m * BLOCK:(m + 1) * BLOCK]


def share_of(me, j, width):
    return pl.ds(pl.multiple_of((me ^ j) * width, width), width)


def add_piece(totals, me, j, x_ref, w_refs):
    width = x_ref.shape[1] // 2
    share = share_of(me, j, width)
    sides = (x_ref[:, :width], x_ref[:, :width], x_ref[:, width:])
    new = [lax.dot_general(x, w[:, share], LAST, preferred_element_type=F32) for x, w in zip(sides, w_refs)]
    return new if totals is None else [t + n for t, n in zip(totals, new)]


def first_kernel(me_ref, raw_ref, wg_ref, wu_ref, wd_ref, own_ref, *outs):
    unpack(mover(), raw_ref, own_ref)
    totals = add_piece(None, me_ref[0], 0, own_ref, (wg_ref, wu_ref, wd_ref))
    for out, total in zip(outs, totals):
        out[...] = total


def chip_kernel(me_ref, core_ref, raw_ref, wg_ref, wu_ref, wd_ref, a_ref, b_ref, c_ref, chip_ref, *outs):
    unpack(mover(), raw_ref, chip_ref)
    totals = [a_ref[...], b_ref[...], c_ref[...]]
    totals = add_piece(totals, me_ref[0], 1, core_ref, (wg_ref, wu_ref, wd_ref))
    totals = add_piece(totals, me_ref[0], 2, chip_ref, (wg_ref, wu_ref, wd_ref))
    for out, total in zip(outs, totals):
        out[...] = total


def terms_kernel(me_ref, raw_ref, wg_ref, wu_ref, wd_ref, a_ref, b_ref, c_ref,
                 keep_ref, send_ref, hid_ref, ggp_ref, gup_ref, sum_ref, far_out, far_ref, sem):
    rows, both = far_ref.shape
    width = both // 2
    me = me_ref[0]
    unpack(mover(), raw_ref, far_ref)
    copy = pltpu.make_async_copy(far_ref, far_out, sem)
    copy.start()
    totals = [a_ref[...], b_ref[...], c_ref[...]]
    pre_gate, pre_up, hid_grad = add_piece(totals, me, 3, far_ref, (wg_ref, wu_ref, wd_ref))
    sigma = jax.nn.sigmoid(pre_gate)
    swish = pre_gate * sigma
    hidden = (swish * pre_up).astype(BF16)
    ggp = (hid_grad * pre_up * sigma * (1.0 + pre_gate * (1.0 - sigma))).astype(BF16)
    gup = (hid_grad * swish).astype(BF16)
    hid_ref[...] = hidden
    ggp_ref[...] = ggp
    gup_ref[...] = gup
    gate = jnp.sum(hidden.astype(F32) * hid_grad, axis=1, keepdims=True)
    count = rows // CAP
    lane = iota((count, LANES), 1)
    table = jnp.zeros((count, LANES), F32)
    for c in range(CAP):
        table = jnp.where(lane == c, gate[c * count:(c + 1) * count], table)
    table = table.astype(BF16)
    tall = count * LANES // width
    for q in range(width // LANES):
        sum_ref[:, q * LANES:(q + 1) * LANES] = table[q * tall:(q + 1) * tall]
    for j, out_ref in ((3, send_ref), (2, keep_ref)):
        put_terms(me, j, ggp, gup, wg_ref, wu_ref, sum_ref, out_ref)
    copy.wait()


def put_terms(me, j, ggp, gup, wg_ref, wu_ref, sum_ref, out_ref):
    rows, width = ggp.shape[0], out_ref.shape[1]
    share = share_of(me, j, width)
    terms = jnp.dot(ggp, wg_ref[:, share], preferred_element_type=F32)
    terms = terms + jnp.dot(gup, wu_ref[:, share], preferred_element_type=F32)
    out_ref[:rows, :] = terms.astype(BF16)
    out_ref[rows:, :] = sum_ref[...]


def near_kernel(me_ref, ggp_ref, gup_ref, wg_ref, wu_ref, sum_ref, keep_ref, send_ref):
    for j, out_ref in ((1, send_ref), (0, keep_ref)):
        put_terms(me_ref[0], j, ggp_ref[...], gup_ref[...], wg_ref, wu_ref, sum_ref, out_ref)


def weight_kernel(me_ref, own_ref, core_ref, chip_ref, far_ref, hid_ref, ggp_ref, gup_ref,
                  wg_out, wu_out, wd_out):
    width = own_ref.shape[1] // 2
    hid, ggp, gup = hid_ref[...].T, ggp_ref[...].T, gup_ref[...].T
    for j, x_ref in enumerate((own_ref, core_ref, chip_ref, far_ref)):
        share = share_of(me_ref[0], j, width)
        acts = x_ref[:, :width]
        grad = x_ref[:, width:]
        wg_out[:, share] = jnp.dot(ggp, acts, preferred_element_type=F32).astype(BF16)
        wu_out[:, share] = jnp.dot(gup, acts, preferred_element_type=F32).astype(BF16)
        wd_out[:, share] = jnp.dot(hid, grad, preferred_element_type=F32).astype(BF16)


def back_kernel(sum_ref, core_ref, out_ref):
    wide, width = sum_ref.shape
    chunks = width // LANES
    experts = out_ref.shape[0] // BLOCK
    rows = CAP * experts
    tall = wide - rows
    total = (sum_ref[...].astype(F32) + core_ref[...].astype(F32)).astype(BF16)
    table = [total[rows:, q * LANES:(q + 1) * LANES] for q in range(chunks)]
    size = BLOCK * BLOCK
    taken = (chunks * CAP + 1) * BLOCK
    line = low(iota((size, taken), 0), BLOCK)
    source = high(iota((size, taken), 0), BLOCK)
    wanted = jnp.where(
        line < chunks * CAP,
        (low(line, chunks) * CAP + high(line, chunks)) * BLOCK + source,
        jnp.where(line == chunks * CAP, chunks * CAP * BLOCK + source, -1),
    )
    move = (wanted == iota((size, taken), 1)).astype(BF16)
    for b in range(experts // BLOCK):
        parts = [
            total[c * experts + b * BLOCK:c * experts + (b + 1) * BLOCK, i * LANES:(i + 1) * LANES]
            for i in range(chunks) for c in range(CAP)
        ]
        start = b * BLOCK % tall
        parts.append(table[b * BLOCK // tall][start:start + BLOCK])
        data = jnp.concatenate(parts, axis=0)
        out_ref[b * size:(b + 1) * size, :] = jnp.dot(
            move, data, preferred_element_type=F32
        ).astype(BF16)


def token_kernel(idx_ref, gate_ref, back_ref, acts_ref, gate_out):
    tokens, width = acts_ref.shape
    chunks = width // LANES
    experts = back_ref.shape[0] // BLOCK
    hits, slot, _ = routes(idx_ref[...], gate_ref[...], experts, chunks)
    lanes = chunks * tokens
    code = jnp.where(
        slot < 0.0, -1, slot.astype(jnp.int32) * chunks + high(iota((experts, lanes), 1), tokens)
    )
    line = iota((experts, BLOCK, lanes), 1)
    place = jnp.where(code[:, None, :] == line, 1.0, 0.0).astype(BF16).reshape(experts * BLOCK, lanes)
    back = back_ref[...]
    made = lax.dot_general(place, back, FIRST, preferred_element_type=F32).astype(BF16)
    for q in range(chunks):
        acts_ref[:, q * LANES:(q + 1) * LANES] = made[q * tokens:(q + 1) * tokens]
    spot = iota((experts, experts * BLOCK), 0) * BLOCK + chunks * CAP
    pick = (iota((experts, experts * BLOCK), 1) == spot).astype(BF16)
    sums = jnp.dot(pick, back, preferred_element_type=F32)
    chosen = jnp.zeros((experts, lanes), F32)
    for c in range(CAP):
        chosen = jnp.where(slot == float(c), sums[:, c:c + 1], chosen)
    gates = [jnp.sum(jnp.where(hit, chosen, 0.0), axis=0, keepdims=True) for hit in hits]
    gates = jnp.concatenate(gates, axis=0)[:, :tokens]
    gate_out[...] = (gates / gate_ref[...].astype(F32)).astype(BF16)


VMEM = pl.BlockSpec(memory_space=pltpu.VMEM)
HBM = pl.BlockSpec(memory_space=pltpu.HBM)
SMEM = pl.BlockSpec(memory_space=pltpu.SMEM)


def call(kernel, outs, flops, args, scalars=0, scratch=(), space=VMEM, limit=16, kept=0):
    moved = sum(a.size * a.dtype.itemsize for a in args)
    moved += sum(o.size * o.dtype.itemsize for o in outs)
    return pl.pallas_call(
        kernel,
        out_shape=outs,
        in_specs=[SMEM] * scalars + [space] * (len(args) - scalars),
        out_specs=[space] * (len(outs) - kept) + [HBM] * kept,
        scratch_shapes=list(scratch),
        cost_estimate=pl.CostEstimate(flops=flops, bytes_accessed=moved, transcendentals=0),
        compiler_params=pltpu.CompilerParams(vmem_limit_bytes=limit << 20),
    )(*args)


def shape(dims, dtype=BF16):
    return jax.ShapeDtypeStruct(dims, dtype)


def body(acts, grad_out, experts_idx, gate_prob, w_gate, w_up, w_down):
    tokens, top = experts_idx.shape
    width = acts.shape[1]
    experts = lax.axis_size(GROUP)
    rows = CAP * experts
    units, features = w_gate.shape[1:]
    me = lax.axis_index("rep").astype(jnp.int32).reshape(1)
    weights = (w_gate[0], w_up[0], w_down[0])
    idx, gate = experts_idx.T, gate_prob.T

    lines = CAP * 2 * width // LANES
    lanes = 2 * width // LANES * tokens
    (send,) = call(
        send_kernel, [shape((experts * lines, LANES))], 2 * experts * lines * lanes * LANES,
        (idx, gate, acts, grad_out),
        scratch=(
            pltpu.VMEM((experts, lanes), jnp.int32),
            pltpu.VMEM((experts, lanes), F32),
            pltpu.VMEM(idx.shape, idx.dtype),
            pltpu.VMEM(gate.shape, gate.dtype),
            pltpu.VMEM(acts.shape, BF16),
            pltpu.VMEM(acts.shape, BF16),
            pltpu.VMEM((experts // BLOCK, BLOCK * lines, LANES), BF16),
            pltpu.SemaphoreType.DMA((4 + experts // BLOCK,)),
        ),
        space=HBM, limit=56,
    )
    got = lax.all_to_all(
        send.reshape(experts, lines, LANES), GROUP, split_axis=0, concat_axis=0, tiled=True
    ).reshape(experts * lines, LANES)
    chip_raw = swap(got, 2)
    product = 2 * rows * units * width
    sums = [shape((rows, units), F32)] * 3
    held = shape((rows, 2 * width))
    own, *first = call(first_kernel, [held] + sums, 3 * product, (me, got, *weights), 1)
    core = swap(own, 1)
    chip_raw, *first = lax.optimization_barrier((chip_raw, *first))
    far_raw = swap(chip_raw, 1)
    chip, *third = call(
        chip_kernel, [held] + sums, 6 * product, (me, core, chip_raw, *weights, *first), 1
    )
    tall = experts * LANES // width
    piece = shape((rows + tall, width))
    keep2, send3, hid, ggp, gup, gates, far = call(
        terms_kernel, [piece] * 2 + [shape((rows, units))] * 3 + [shape((tall, width)), held], 7 * product,
        (me, far_raw, *weights, *third), 1,
        scratch=(pltpu.VMEM((rows, 2 * width), BF16), pltpu.SemaphoreType.DMA(())), kept=1,
    )
    half = keep2 + swap(send3, 1)
    came = swap(half, 2)
    keep0, send1 = call(near_kernel, [piece] * 2, 4 * product, (me, ggp, gup, *weights[:2], gates), 1)
    near = swap(send1, 1)
    wg_grad, wu_grad, wd_grad = call(
        weight_kernel, [shape((units, features))] * 3, 12 * product,
        (me, own, core, chip, far, hid, ggp, gup), 1,
    )
    (back,) = call(
        back_kernel, [shape((experts * BLOCK, LANES))], 2 * experts * BLOCK * 256 * LANES,
        (keep0 + came, near),
    )
    back = lax.all_to_all(
        back.reshape(experts, BLOCK, LANES), GROUP, split_axis=0, concat_axis=0, tiled=True
    )
    acts_grad, gate_grad = call(
        token_kernel, [shape((tokens, width)), shape((top, tokens))],
        4 * experts * BLOCK * LANES * LANES,
        (idx, gate, back.reshape(experts * BLOCK, LANES)),
    )
    return (acts_grad, gate_grad.T, wg_grad[None], wu_grad[None], wd_grad[None])


def solution(mesh):
    rows = P(GROUP, "rep")
    table = P(GROUP, None)
    weight = P(GROUP, "rep", None)
    return jax.shard_map(
        body,
        mesh=mesh,
        in_specs=(rows, rows, table, table, weight, weight, weight),
        out_specs=(rows, table, weight, weight, weight),
        check_vma=False,
    )
```

time: 138 us -> 130 us (0.942)
  Pallas kernels: 5.72 us -> 14.6 us
  local copies, waits for them, and re-layouts: 9.95 us -> 1.19 us
  waiting for transfers between devices: 44.2 us -> 40.2 us
  matrix products: 2.82 us -> 0 us
  other arithmetic: 2.97 us -> 0.21 us
  starting transfers between devices: 22.5 us -> 24 us
    pallas_call x2 -> x8, Pallas kernels: 5.72 us -> 14.6 us  [call(): pl.pallas_call(kernel, out_shape=outs, in_specs=[SMEM] * scalars + [space...]
    ppermute x5 -> x6, waiting for transfers between devices: 28.5 us -> 22.7 us  [swap(): lax.ppermute(x, 'rep', [(i, i ^ bit) for i in range(lax.axis_size('rep'))])]
    unnamed x25 -> x26, local copies, waits for them, and re-layouts: 6.11 us -> 1.19 us
    dot_general x5 -> x0, matrix products: 2.82 us -> none  [the longest x1 1.89 us: body(): lax.dot_general(placing, back[:, :cap].reshape(rows, width), FIRST, prefe...]
    ppermute x5 -> x6, starting transfers between devices: 14.3 us -> 16.2 us  [swap(): lax.ppermute(x, 'rep', [(i, i ^ bit) for i in range(lax.axis_size('rep'))])]
    all_to_all x1, waiting for transfers between devices: 15.7 us -> 17.5 us  [body(): lax.all_to_all(back.reshape(experts, BLOCK, LANES), GROUP, split_axis=0,...]
  transfers between devices with their start and end apart: 6 -> 7, of which waited for: 5 -> 4; matrix products, arithmetic and copies ran while one was open for 0% -> 0% of each run, Pallas kernels for 2% -> 6%
where the time goes in v2:
time: 130 us
  blocking collectives  48.5 us (37%)
  waiting for transfers between devices  40.2 us (31%)
  starting transfers between devices  24 us (18%)
  Pallas kernels  14.6 us (11%)
    all_to_all x1, blocking collectives, body(): lax.all_to_all(send.reshape(experts, lines, LANES), GROUP, split_axis=0,...  48.5 us
    ppermute x6, waiting for transfers between devices, swap(): lax.ppermute(x, 'rep', [(i, i ^ bit) for i in range(lax.axis_size('rep'))])  22.7 us
    all_to_all x1, waiting for transfers between devices, body(): lax.all_to_all(back.reshape(experts, BLOCK, LANES), GROUP, split_axis=0,...  17.5 us
    ppermute x6, starting transfers between devices, swap(): lax.ppermute(x, 'rep', [(i, i ^ bit) for i in range(lax.axis_size('rep'))])  16.2 us
    pallas_call x8, Pallas kernels, call(): pl.pallas_call(kernel, out_shape=outs, in_specs=[SMEM] * scalars + [space...  14.6 us
    all_to_all x1, starting transfers between devices, body(): lax.all_to_all(back.reshape(experts, BLOCK, LANES), GROUP, split_axis=0,...  7.77 us
  transfers between devices with their start and end apart: 7, of which 4 were waited for; matrix products, arithmetic and copies ran while one was open for 0% of the time, Pallas kernels for 6%

profile of v2, /device:TPU:1, one launch (start us, length us, event | category | flops | bytes accessed | tf_op | source)
XLA Modules:
  0.0 129.6 jit_solution(1258827435180508067)
XLA Ops:
  0.6 0.0 copy-start.2
  0.6 2.6 %shard_map.110 = bf16[3072,128]{1,0:T(8,128)(2,1)} custom-call(s32[8,32]{1,0:T(8,128)} %bitcast.28, bf16[8,32]{1,0:T(8,128)(2,1)} %bitcast.30, bf16[32,512]{1,0:T(8,128)(2,1)} %refs_2_.1, bf16[32,512]{1,0:T(8,128)(2,1)} %refs_3_.1), custom_call_target="tpu_custom_call" | custom-call | flops 201326592 | bytes 853504 | tf_op jit(solution)/shard_map/pallas_call | solution.py:263
  3.2 0.0 copy-start
  3.2 0.0 copy-start.1
  3.3 48.5 %all_to_all.10 = bf16[128,24,128]{2,1,0:T(8,128)(2,1)S(1)} all-to-all(bf16[128,24,128]{2,1,0:T(8,128)(2,1)} %bitcast.32), channel_id=1, replica_groups=mesh['ctx'=8,'exp'=16,'rep'=4] {'ctx','exp'}, dimensions={0} | all-to-all | bytes 1572864 | tf_op jit(solution)/shard_map/all_to_all | solution.py:305
  51.8 1.9 %collective-permute-start = (bf16[3072,128]{1,0:T(8,128)(2,1)S(1)}, bf16[3072,128]{1,0:T(8,128)(2,1)}, u32[]{:S(2)}, u32[]{:S(2)}) collective-permute-start(bf16[3072,128]{1,0:T(8,128)(2,1)S(1)} %bitcast.25), channel_id=1, source_target_pairs={{0,2},{1,3},{2,0},{3,1},{4,6},{5,7},{6,4},{7,5},{8,10},{9,11},{10,... | collective-permute-start | bytes 2359304 | tf_op jit(solution)/shard_map/ppermute | solution.py:19
  53.7 0.0 copy-done.2
  53.7 0.0 copy-done
  53.7 0.0 copy-done.1
  53.7 1.2 shard_map.111
  54.9 0.0 copy-start.5
  54.9 3.6 %collective-permute-start.2 = (bf16[384,1024]{1,0:T(8,128)(2,1)S(1)}, bf16[384,1024]{1,0:T(8,128)(2,1)S(1)}, u32[]{:S(2)}, u32[]{:S(2)}) collective-permute-start(bf16[384,1024]{1,0:T(8,128)(2,1)S(1)} %get-tuple-element.35.own_ref), channel_id=1, source_target_pairs={{0,1},{1,0},{2,3},{3,2},{4,5},{5,4},{6,7},{7,6},{8,9},{9,8},{10,11... | collective-permute-start | bytes 2359304 | tf_op jit(solution)/shard_map/ppermute | solution.py:19
  58.5 12.6 %collective-permute-done.raw_ref = bf16[3072,128]{1,0:T(8,128)(2,1)} collective-permute-done((bf16[3072,128]{1,0:T(8,128)(2,1)S(1)}, bf16[3072,128]{1,0:T(8,128)(2,1)}, u32[]{:S(2)}, u32[]{:S(2)}) %collective-permute-start) | collective-permute-done | bytes 786464 | tf_op jit(solution)/shard_map/ppermute | solution.py:19
  71.1 4.5 %collective-permute-start.1 = (bf16[3072,128]{1,0:T(8,128)(2,1)}, bf16[3072,128]{1,0:T(8,128)(2,1)S(1)}, u32[]{:S(2)}, u32[]{:S(2)}) collective-permute-start(bf16[3072,128]{1,0:T(8,128)(2,1)} %collective-permute-done.raw_ref), channel_id=1, source_target_pairs={{0,1},{1,0},{2,3},{3,2},{4,5},{5,4},{6,7},{7,6},{8,9},{9,8},{10,11... | collective-permute-start | bytes 2359304 | tf_op jit(solution)/shard_map/ppermute | solution.py:19
  75.6 0.0 collective-permute-done.2.core_ref
  75.6 0.0 copy-start.3
  75.6 2.8 %shard_map.112 = (bf16[384,1024]{1,0:T(8,128)(2,1)S(1)}, f32[384,192]{1,0:T(8,128)S(1)}, f32[384,192]{1,0:T(8,128)S(1)}, f32[384,192]{1,0:T(8,128)S(1)}) custom-call(s32[1]{0:T(128)} %bitcast.2.me_ref, bf16[384,1024]{1,0:T(8,128)(2,1)S(1)} %collective-permute-done.2.core_ref, bf16[3072,128]{1,0:T(8,128)(2,1)} %collective-permute-done.raw_ref, ...), custom_call_target="tpu_custom_call" | custom-call | flops 452984832 | bytes 6488068 | tf_op jit(solution)/shard_map/pallas_call | solution.py:263
  78.5 0.0 copy-done.5
  78.5 0.0 copy-done.3
  78.5 0.0 collective-permute-done.1.raw_ref
  78.5 2.1 %shard_map.113 = (bf16[416,512]{1,0:T(8,128)(2,1)S(1)}, bf16[416,512]{1,0:T(8,128)(2,1)S(1)}, bf16[384,192]{1,0:T(8,128)(2,1)S(1)}, bf16[384,192]{1,0:T(8,128)(2...) custom-call(s32[1]{0:T(128)} %bitcast.2.me_ref, ...), custom_call_target="tpu_custom_call" | custom-call | flops 528482304 | bytes 6144004 | tf_op jit(solution)/shard_map/pallas_call | solution.py:263
  80.6 0.0 copy-start.9
  80.6 0.0 copy-start.7
  80.6 1.9 %collective-permute-start.3 = (bf16[416,512]{1,0:T(8,128)(2,1)S(1)}, bf16[416,512]{1,0:T(8,128)(2,1)S(1)}, u32[]{:S(2)}, u32[]{:S(2)}) collective-permute-start(bf16[416,512]{1,0:T(8,128)(2,1)S(1)} %get-tuple-element.47), channel_id=1, source_target_pairs={{0,1},{1,0},{2,3},{3,2},{4,5},{5,4},{6,7},{7,6},{8,9},{9,8},{10,11... | collective-permute-start | bytes 1277960 | tf_op jit(solution)/shard_map/ppermute | solution.py:19
  82.6 1.7 %collective-permute-done.3 = bf16[416,512]{1,0:T(8,128)(2,1)S(1)} collective-permute-done((bf16[416,512]{1,0:T(8,128)(2,1)S(1)}, bf16[416,512]{1,0:T(8,128)(2,1)S(1)}, u32[]{:S(2)}, u32[]{:S(2)}) %collective-permute-start.3) | collective-permute-done | bytes 426016 | tf_op jit(solution)/shard_map/ppermute | solution.py:19
  84.3 0.1 add.6
  84.4 0.0 copy-done.9
  84.4 1.9 %collective-permute-start.4 = (bf16[416,512]{1,0:T(8,128)(2,1)S(1)}, bf16[416,512]{1,0:T(8,128)(2,1)S(1)}, u32[]{:S(2)}, u32[]{:S(2)}) collective-permute-start(bf16[416,512]{1,0:T(8,128)(2,1)S(1)} %add.6), channel_id=1, source_target_pairs={{0,2},{1,3},{2,0},{3,1},{4,6},{5,7},{6,4},{7,5},{8,10},{9,11},{10,... | collective-permute-start | bytes 1277960 | tf_op jit(solution)/shard_map/ppermute | solution.py:19
  86.4 0.6 shard_map.114
  86.9 0.0 copy-done.7
  86.9 2.3 %collective-permute-start.5 = (bf16[416,512]{1,0:T(8,128)(2,1)S(1)}, bf16[416,512]{1,0:T(8,128)(2,1)S(1)}, u32[]{:S(2)}, u32[]{:S(2)}) collective-permute-start(bf16[416,512]{1,0:T(8,128)(2,1)S(1)} %get-tuple-element.48), channel_id=1, source_target_pairs={{0,1},{1,0},{2,3},{3,2},{4,5},{5,4},{6,7},{7,6},{8,9},{9,8},{10,11... | collective-permute-start | bytes 1277960 | tf_op jit(solution)/shard_map/ppermute | solution.py:19
  89.3 8.3 %collective-permute-done.4 = bf16[416,512]{1,0:T(8,128)(2,1)S(1)} collective-permute-done((bf16[416,512]{1,0:T(8,128)(2,1)S(1)}, bf16[416,512]{1,0:T(8,128)(2,1)S(1)}, u32[]{:S(2)}, u32[]{:S(2)}) %collective-permute-start.4) | collective-permute-done | bytes 426016 | tf_op jit(solution)/shard_map/ppermute | solution.py:19
  97.6 0.1 add.7.sum_ref
  97.7 0.0 collective-permute-done.5.core_ref
  97.7 0.0 copy-start.6
  97.7 1.3 shard_map.115
  99.0 0.0 copy-start.4
  99.0 7.8 %all-to-all-start.1 = ((bf16[128,16,128]{2,1,0:T(8,128)(2,1)}), bf16[128,16,128]{2,1,0:T(8,128)(2,1)S(1)}, u32[]{:S(2)}, u32[]{:S(2)}) async-start(bf16[128,16,128]{2,1,0:T(8,128)(2,1)} %bitcast.8), calls=%async_computation.1 | async-start | bytes 1048576 | tf_op jit(solution)/shard_map/all_to_all | solution.py:338
  106.8 0.0 copy-done.6
  106.8 0.0 copy-done.4
  106.8 0.0 copy-done.10
  106.8 0.0 copy-start.8
  106.8 1.1 copy-done.8
  108.0 2.6 %shard_map.117 = (bf16[192,2048]{1,0:T(8,128)(2,1)}, bf16[192,2048]{1,0:T(8,128)(2,1)}, bf16[192,2048]{1,0:T(8,128)(2,1)}) custom-call(s32[1]{0:T(128)} %bitcast.2.me_ref, bf16[384,1024]{1,0:T(8,128)(2,1)S(1)} %copy-done.6, bf16[384,1024]{1,0:T(8,128)(2,1)S(1)} %copy-done.4, bf16[384,1024]{1,0:T(8,128)(2,1)S(1)} %get-tuple-element.51.chip_ref, ...), custom_call_target="tpu_custom_call" | custom-call | flops 905969664 | bytes 5947396 | tf_op jit(solution)/shard_map/pallas_call | solution.py:263
  110.6 17.5 %all-to-all-done.1 = bf16[128,16,128]{2,1,0:T(8,128)(2,1)S(1)} async-done(((bf16[128,16,128]{2,1,0:T(8,128)(2,1)}), bf16[128,16,128]{2,1,0:T(8,128)(2,1)S(1)}, u32[]{:S(2)}, u32[]{:S(2)}) %all-to-all-start.1) | async-done | bytes 524320 | tf_op jit(solution)/shard_map/all_to_all | solution.py:338
  128.1 0.0 copy-done.11
  128.1 0.0 copy-done.12
  128.1 1.5 %shard_map.116 = (bf16[32,512]{1,0:T(8,128)(2,1)}, bf16[8,32]{1,0:T(8,128)(2,1)}) custom-call(s32[8,32]{1,0:T(8,128)S(1)} %bitcast.29, bf16[8,32]{1,0:T(8,128)(2,1)S(1)} %bitcast.31, bf16[2048,128]{1,0:T(8,128)(2,1)S(1)} %bitcast.27), custom_call_target="tpu_custom_call" | custom-call | flops 134217728 | bytes 559104 | tf_op jit(solution)/shard_map/pallas_call | solution.py:263
  (3 shorter events, 0.0 us)
Async XLA Ops:
  0.6 53.1 %copy-start.2 = (bf16[1,192,2048]{2,1,0:T(8,128)(2,1)S(1)}, bf16[1,192,2048]{2,1,0:T(8,128)(2,1)}, u32[]{:S(2)}) copy-start(bf16[1,192,2048]{2,1,0:T(8,128)(2,1)} %param.13) | copy-start | bytes 2359300
  3.2 50.5 %copy-start = (bf16[1,192,2048]{2,1,0:T(8,128)(2,1)S(1)}, bf16[1,192,2048]{2,1,0:T(8,128)(2,1)}, u32[]{:S(2)}) copy-start(bf16[1,192,2048]{2,1,0:T(8,128)(2,1)} %param.11) | copy-start | bytes 2359300
  3.2 50.5 %copy-start.1 = (bf16[1,192,2048]{2,1,0:T(8,128)(2,1)S(1)}, bf16[1,192,2048]{2,1,0:T(8,128)(2,1)}, u32[]{:S(2)}) copy-start(bf16[1,192,2048]{2,1,0:T(8,128)(2,1)} %param.12) | copy-start | bytes 2359300
  51.8 19.3 %collective-permute-start = (bf16[3072,128]{1,0:T(8,128)(2,1)S(1)}, bf16[3072,128]{1,0:T(8,128)(2,1)}, u32[]{:S(2)}, u32[]{:S(2)}) collective-permute-start(bf16[3072,128]{1,0:T(8,128)(2,1)S(1)} %bitcast.25), channel_id=1, source_target_pairs={{0,2},{1,3},{2,0},{3,1},{4,6},{5,7},{6,4},{7,5},{8,10},{9,11},{10,... | collective-permute-start | bytes 2359304 | tf_op jit(solution)/shard_map/ppermute | solution.py:19
  54.9 23.6 %copy-start.5 = (bf16[384,1024]{1,0:T(8,128)(2,1)}, bf16[384,1024]{1,0:T(8,128)(2,1)S(1)}, u32[]{:S(2)}) copy-start(bf16[384,1024]{1,0:T(8,128)(2,1)S(1)} %get-tuple-element.35.own_ref) | copy-start | bytes 2359300
  54.9 20.7 %collective-permute-start.2 = (bf16[384,1024]{1,0:T(8,128)(2,1)S(1)}, bf16[384,1024]{1,0:T(8,128)(2,1)S(1)}, u32[]{:S(2)}, u32[]{:S(2)}) collective-permute-start(bf16[384,1024]{1,0:T(8,128)(2,1)S(1)} %get-tuple-element.35.own_ref), channel_id=1, source_target_pairs={{0,1},{1,0},{2,3},{3,2},{4,5},{5,4},{6,7},{7,6},{8,9},{9,8},{10,11... | collective-permute-start | bytes 2359304 | tf_op jit(solution)/shard_map/ppermute | solution.py:19
  71.1 7.4 %collective-permute-start.1 = (bf16[3072,128]{1,0:T(8,128)(2,1)}, bf16[3072,128]{1,0:T(8,128)(2,1)S(1)}, u32[]{:S(2)}, u32[]{:S(2)}) collective-permute-start(bf16[3072,128]{1,0:T(8,128)(2,1)} %collective-permute-done.raw_ref), channel_id=1, source_target_pairs={{0,1},{1,0},{2,3},{3,2},{4,5},{5,4},{6,7},{7,6},{8,9},{9,8},{10,11... | collective-permute-start | bytes 2359304 | tf_op jit(solution)/shard_map/ppermute | solution.py:19
  75.6 2.9 %copy-start.3 = (bf16[384,1024]{1,0:T(8,128)(2,1)}, bf16[384,1024]{1,0:T(8,128)(2,1)S(1)}, u32[]{:S(2)}) copy-start(bf16[384,1024]{1,0:T(8,128)(2,1)S(1)} %collective-permute-done.2.core_ref) | copy-start | bytes 2359300
  80.6 3.8 %copy-start.9 = (bf16[384,192]{1,0:T(8,128)(2,1)}, bf16[384,192]{1,0:T(8,128)(2,1)S(1)}, u32[]{:S(2)}) copy-start(bf16[384,192]{1,0:T(8,128)(2,1)S(1)} %get-tuple-element.53.hid_ref) | copy-start | bytes 442372
  80.6 6.3 %copy-start.7 = (bf16[384,1024]{1,0:T(8,128)(2,1)}, bf16[384,1024]{1,0:T(8,128)(2,1)S(1)}, u32[]{:S(2)}) copy-start(bf16[384,1024]{1,0:T(8,128)(2,1)S(1)} %get-tuple-element.52.far_ref) | copy-start | bytes 2359300
  80.6 3.7 %collective-permute-start.3 = (bf16[416,512]{1,0:T(8,128)(2,1)S(1)}, bf16[416,512]{1,0:T(8,128)(2,1)S(1)}, u32[]{:S(2)}, u32[]{:S(2)}) collective-permute-start(bf16[416,512]{1,0:T(8,128)(2,1)S(1)} %get-tuple-element.47), channel_id=1, source_target_pairs={{0,1},{1,0},{2,3},{3,2},{4,5},{5,4},{6,7},{7,6},{8,9},{9,8},{10,11... | collective-permute-start | bytes 1277960 | tf_op jit(solution)/shard_map/ppermute | solution.py:19
  84.4 13.2 %collective-permute-start.4 = (bf16[416,512]{1,0:T(8,128)(2,1)S(1)}, bf16[416,512]{1,0:T(8,128)(2,1)S(1)}, u32[]{:S(2)}, u32[]{:S(2)}) collective-permute-start(bf16[416,512]{1,0:T(8,128)(2,1)S(1)} %add.6), channel_id=1, source_target_pairs={{0,2},{1,3},{2,0},{3,1},{4,6},{5,7},{6,4},{7,5},{8,10},{9,11},{10,... | collective-permute-start | bytes 1277960 | tf_op jit(solution)/shard_map/ppermute | solution.py:19
  86.9 10.8 %collective-permute-start.5 = (bf16[416,512]{1,0:T(8,128)(2,1)S(1)}, bf16[416,512]{1,0:T(8,128)(2,1)S(1)}, u32[]{:S(2)}, u32[]{:S(2)}) collective-permute-start(bf16[416,512]{1,0:T(8,128)(2,1)S(1)} %get-tuple-element.48), channel_id=1, source_target_pairs={{0,1},{1,0},{2,3},{3,2},{4,5},{5,4},{6,7},{7,6},{8,9},{9,8},{10,11... | collective-permute-start | bytes 1277960 | tf_op jit(solution)/shard_map/ppermute | solution.py:19
  97.7 9.1 %copy-start.6 = (bf16[384,1024]{1,0:T(8,128)(2,1)S(1)}, bf16[384,1024]{1,0:T(8,128)(2,1)}, u32[]{:S(2)}) copy-start(bf16[384,1024]{1,0:T(8,128)(2,1)} %copy-done.5) | copy-start | bytes 2359300
  99.0 7.8 %copy-start.4 = (bf16[384,1024]{1,0:T(8,128)(2,1)S(1)}, bf16[384,1024]{1,0:T(8,128)(2,1)}, u32[]{:S(2)}) copy-start(bf16[384,1024]{1,0:T(8,128)(2,1)} %copy-done.3) | copy-start | bytes 2359300
  99.0 7.8 %copy-start.10 = (bf16[384,192]{1,0:T(8,128)(2,1)S(1)}, bf16[384,192]{1,0:T(8,128)(2,1)}, u32[]{:S(2)}) copy-start(bf16[384,192]{1,0:T(8,128)(2,1)} %copy-done.9) | copy-start | bytes 442372
  99.0 29.1 %all-to-all-start.1 = ((bf16[128,16,128]{2,1,0:T(8,128)(2,1)}), bf16[128,16,128]{2,1,0:T(8,128)(2,1)S(1)}, u32[]{:S(2)}, u32[]{:S(2)}) async-start(bf16[128,16,128]{2,1,0:T(8,128)(2,1)} %bitcast.8), calls=%async_computation.1 | async-start | bytes 1048576 | tf_op jit(solution)/shard_map/all_to_all | solution.py:338
  106.8 1.1 copy-start.8
  108.0 20.1 %copy-start.11 = (s32[32,8]{0,1:T(8,128)S(1)}, s32[32,8]{0,1:T(8,128)}, u32[]{:S(2)}) copy-start(s32[32,8]{0,1:T(8,128)} %param.9) | copy-start | bytes 3076
  108.0 20.1 %copy-start.12 = (bf16[32,8]{0,1:T(8,128)(2,1)S(1)}, bf16[32,8]{0,1:T(8,128)(2,1)}, u32[]{:S(2)}) copy-start(bf16[32,8]{0,1:T(8,128)(2,1)} %param.10) | copy-start | bytes 1540

commit v3 on v2

--- a/solution.py
+++ b/solution.py
@@ -96,15 +96,19 @@
     return (low(out, BLOCK) * lines + high(out, BLOCK) == line).astype(BF16)
 
 
-def unpack(move, raw_ref, out_ref):
+def unpack_kernel(raw_ref, out_ref):
+    move = mover()
     size = move.shape[0]
     chunks = out_ref.shape[1] // LANES
     sources = raw_ref.shape[0] // size * BLOCK
-    for b in range(sources // BLOCK):
-        made = jnp.dot(move, raw_ref[b * size:(b + 1) * size, :], preferred_element_type=F32).astype(BF16)
+    for b in range(0, sources // BLOCK, 2):
+        pair = [raw_ref[(b + n) * size:(b + n + 1) * size, :] for n in range(2)]
+        made = jnp.dot(move, jnp.concatenate(pair, axis=1), preferred_element_type=F32).astype(BF16)
         for m in range(size // BLOCK):
-            row, lane = m // chunks * sources + b * BLOCK, m % chunks * LANES
-            out_ref[row:row + BLOCK, lane:lane + LANES] = made[m * BLOCK:(m + 1) * BLOCK]
+            for n in range(2):
+                row, lane = m // chunks * sources + (b + n) * BLOCK, m % chunks * LANES
+                part = made[m * BLOCK:(m + 1) * BLOCK, n * LANES:(n + 1) * LANES]
+                out_ref[row:row + BLOCK, lane:lane + LANES] = part
 
 
 def share_of(me, j, width):
@@ -119,15 +123,13 @@
     return new if totals is None else [t + n for t, n in zip(totals, new)]
 
 
-def first_kernel(me_ref, raw_ref, wg_ref, wu_ref, wd_ref, own_ref, *outs):
-    unpack(mover(), raw_ref, own_ref)
+def first_kernel(me_ref, own_ref, wg_ref, wu_ref, wd_ref, *outs):
     totals = add_piece(None, me_ref[0], 0, own_ref, (wg_ref, wu_ref, wd_ref))
     for out, total in zip(outs, totals):
         out[...] = total
 
 
-def chip_kernel(me_ref, core_ref, raw_ref, wg_ref, wu_ref, wd_ref, a_ref, b_ref, c_ref, chip_ref, *outs):
-    unpack(mover(), raw_ref, chip_ref)
+def second_kernel(me_ref, core_ref, chip_ref, wg_ref, wu_ref, wd_ref, a_ref, b_ref, c_ref, *outs):
     totals = [a_ref[...], b_ref[...], c_ref[...]]
     totals = add_piece(totals, me_ref[0], 1, core_ref, (wg_ref, wu_ref, wd_ref))
     totals = add_piece(totals, me_ref[0], 2, chip_ref, (wg_ref, wu_ref, wd_ref))
@@ -135,14 +137,11 @@
         out[...] = total
 
 
-def terms_kernel(me_ref, raw_ref, wg_ref, wu_ref, wd_ref, a_ref, b_ref, c_ref,
-                 keep_ref, send_ref, hid_ref, ggp_ref, gup_ref, sum_ref, far_out, far_ref, sem):
+def terms_kernel(me_ref, far_ref, wg_ref, wu_ref, wd_ref, a_ref, b_ref, c_ref,
+                 keep_ref, send_ref, hid_ref, ggp_ref, gup_ref, sum_ref):
     rows, both = far_ref.shape
     width = both // 2
     me = me_ref[0]
-    unpack(mover(), raw_ref, far_ref)
-    copy = pltpu.make_async_copy(far_ref, far_out, sem)
-    copy.start()
     totals = [a_ref[...], b_ref[...], c_ref[...]]
     pre_gate, pre_up, hid_grad = add_piece(totals, me, 3, far_ref, (wg_ref, wu_ref, wd_ref))
     sigma = jax.nn.sigmoid(pre_gate)
@@ -165,7 +164,6 @@
         sum_ref[:, q * LANES:(q + 1) * LANES] = table[q * tall:(q + 1) * tall]
     for j, out_ref in ((3, send_ref), (2, keep_ref)):
         put_terms(me, j, ggp, gup, wg_ref, wu_ref, sum_ref, out_ref)
-    copy.wait()
 
 
 def put_terms(me, j, ggp, gup, wg_ref, wu_ref, sum_ref, out_ref):
@@ -195,7 +193,7 @@
         wd_out[:, share] = jnp.dot(hid, grad, preferred_element_type=F32).astype(BF16)
 
 
-def back_kernel(sum_ref, core_ref, out_ref):
+def back_kernel(sum_ref, core_ref, out_ref, made_ref, sems):
     wide, width = sum_ref.shape
     chunks = width // LANES
     experts = out_ref.shape[0] // BLOCK
@@ -213,41 +211,67 @@
         jnp.where(line == chunks * CAP, chunks * CAP * BLOCK + source, -1),
     )
     move = (wanted == iota((size, taken), 1)).astype(BF16)
-    for b in range(experts // BLOCK):
-        parts = [
-            total[c * experts + b * BLOCK:c * experts + (b + 1) * BLOCK, i * LANES:(i + 1) * LANES]
-            for i in range(chunks) for c in range(CAP)
-        ]
-        start = b * BLOCK % tall
-        parts.append(table[b * BLOCK // tall][start:start + BLOCK])
-        data = jnp.concatenate(parts, axis=0)
-        out_ref[b * size:(b + 1) * size, :] = jnp.dot(
-            move, data, preferred_element_type=F32
+    copies = []
+    for b in range(0, experts // BLOCK, 2):
+        pair = []
+        for d in (b, b + 1):
+            parts = [
+                total[c * experts + d * BLOCK:c * experts + (d + 1) * BLOCK, i * LANES:(i + 1) * LANES]
+                for i in range(chunks) for c in range(CAP)
+            ]
+            start = d * BLOCK % tall
+            parts.append(table[d * BLOCK // tall][start:start + BLOCK])
+            pair.append(jnp.concatenate(parts, axis=0))
+        made = jnp.dot(
+            move, jnp.concatenate(pair, axis=1), preferred_element_type=F32
         ).astype(BF16)
-
-
-def token_kernel(idx_ref, gate_ref, back_ref, acts_ref, gate_out):
+        for n in range(2):
+            made_ref[b + n] = made[:, n * LANES:(n + 1) * LANES]
+            copies.append(pltpu.make_async_copy(
+                made_ref.at[b + n], out_ref.at[(b + n) * size:(b + n + 1) * size, :], sems.at[b + n]
+            ))
+            copies[-1].start()
+    for copy in copies:
+        copy.wait()
+
+
+def place_kernel(idx_ref, gate_ref, place_ref, slot_ref, name_ref):
+    top, tokens = idx_ref.shape
+    experts, lanes = slot_ref.shape
+    chunks = lanes // tokens
+    _, slot, _ = routes(idx_ref[...], gate_ref[...], experts, chunks)
+    slot_ref[...] = slot
+    repeat = (low(iota((tokens, lanes), 1), tokens) == iota((tokens, lanes), 0)).astype(F32)
+    name_ref[...] = jnp.dot(idx_ref[...].astype(F32), repeat, preferred_element_type=F32).astype(jnp.int32)
+    code = jnp.where(
+        slot < 0.0, -1, slot.astype(jnp.int32) * chunks + high(iota((experts, lanes), 1), tokens)
+    )
+    line = iota((experts, BLOCK, lanes), 1)
+    place = jnp.where(code[:, None, :] == line, 1.0, 0.0).reshape(experts * BLOCK, lanes)
+    place_ref[:lanes, :] = place.T.astype(BF16)
+    spot = iota((experts, experts * BLOCK), 0) * BLOCK + chunks * CAP
+    place_ref[lanes:, :] = (iota((experts, experts * BLOCK), 1) == spot).astype(BF16)
+
+
+def token_kernel(place_ref, slot_ref, name_ref, gate_ref, back_ref, acts_ref, gate_out):
     tokens, width = acts_ref.shape
     chunks = width // LANES
-    experts = back_ref.shape[0] // BLOCK
-    hits, slot, _ = routes(idx_ref[...], gate_ref[...], experts, chunks)
-    lanes = chunks * tokens
-    code = jnp.where(
-        slot < 0.0, -1, slot.astype(jnp.int32) * chunks + high(iota((experts, lanes), 1), tokens)
-    )
-    line = iota((experts, BLOCK, lanes), 1)
-    place = jnp.where(code[:, None, :] == line, 1.0, 0.0).astype(BF16).reshape(experts * BLOCK, lanes)
-    back = back_ref[...]
-    made = lax.dot_general(place, back, FIRST, preferred_element_type=F32).astype(BF16)
+    experts, lanes = slot_ref.shape
+    made = jnp.dot(place_ref[...], back_ref[...], preferred_element_type=F32)
+    acts = made[:lanes].astype(BF16)
     for q in range(chunks):
-        acts_ref[:, q * LANES:(q + 1) * LANES] = made[q * tokens:(q + 1) * tokens]
-    spot = iota((experts, experts * BLOCK), 0) * BLOCK + chunks * CAP
-    pick = (iota((experts, experts * BLOCK), 1) == spot).astype(BF16)
-    sums = jnp.dot(pick, back, preferred_element_type=F32)
+        acts_ref[:, q * LANES:(q + 1) * LANES] = acts[q * tokens:(q + 1) * tokens]
+    sums = made[lanes:]
+    slot = slot_ref[...]
     chosen = jnp.zeros((experts, lanes), F32)
     for c in range(CAP):
         chosen = jnp.where(slot == float(c), sums[:, c:c + 1], chosen)
-    gates = [jnp.sum(jnp.where(hit, chosen, 0.0), axis=0, keepdims=True) for hit in hits]
+    label = iota((experts, lanes), 0)
+    name = name_ref[...]
+    gates = [
+        jnp.sum(jnp.where(name[k:k + 1] == label, chosen, 0.0), axis=0, keepdims=True)
+        for k in range(name.shape[0])
+    ]
     gates = jnp.concatenate(gates, axis=0)[:, :tokens]
     gate_out[...] = (gates / gate_ref[...].astype(F32)).astype(BF16)
 
@@ -305,23 +329,21 @@
     got = lax.all_to_all(
         send.reshape(experts, lines, LANES), GROUP, split_axis=0, concat_axis=0, tiled=True
     ).reshape(experts * lines, LANES)
-    chip_raw = swap(got, 2)
+    held = shape((rows, 2 * width))
+    (own,) = call(unpack_kernel, [held], 2 * rows * 384 * 2 * width, (got,))
+    chip = swap(own, 2)
+    core = swap(own, 1)
     product = 2 * rows * units * width
     sums = [shape((rows, units), F32)] * 3
-    held = shape((rows, 2 * width))
-    own, *first = call(first_kernel, [held] + sums, 3 * product, (me, got, *weights), 1)
-    core = swap(own, 1)
-    chip_raw, *first = lax.optimization_barrier((chip_raw, *first))
-    far_raw = swap(chip_raw, 1)
-    chip, *third = call(
-        chip_kernel, [held] + sums, 6 * product, (me, core, chip_raw, *weights, *first), 1
-    )
+    first = call(first_kernel, sums, 3 * product, (me, own, *weights), 1)
+    chip, *first = lax.optimization_barrier((chip, *first))
+    far = swap(chip, 1)
+    second = call(second_kernel, sums, 6 * product, (me, core, chip, *weights, *first), 1)
     tall = experts * LANES // width
     piece = shape((rows + tall, width))
-    keep2, send3, hid, ggp, gup, gates, far = call(
-        terms_kernel, [piece] * 2 + [shape((rows, units))] * 3 + [shape((tall, width)), held], 7 * product,
-        (me, far_raw, *weights, *third), 1,
-        scratch=(pltpu.VMEM((rows, 2 * width), BF16), pltpu.SemaphoreType.DMA(())), kept=1,
+    keep2, send3, hid, ggp, gup, gates = call(
+        terms_kernel, [piece] * 2 + [shape((rows, units))] * 3 + [shape((tall, width))], 7 * product,
+        (me, far, *weights, *second), 1,
     )
     half = keep2 + swap(send3, 1)
     came = swap(half, 2)
@@ -331,9 +353,23 @@
         weight_kernel, [shape((units, features))] * 3, 12 * product,
         (me, own, core, chip, far, hid, ggp, gup), 1,
     )
+    summed = keep0 + came
     (back,) = call(
-        back_kernel, [shape((experts * BLOCK, LANES))], 2 * experts * BLOCK * 256 * LANES,
-        (keep0 + came, near),
+        back_kernel, [shape((experts * BLOCK, LANES))], 2 * experts * BLOCK * 256 * LANES, (summed, near),
+        scratch=(
+            pltpu.VMEM((experts // BLOCK, BLOCK * BLOCK, LANES), BF16),
+            pltpu.SemaphoreType.DMA((experts // BLOCK,)),
+        ),
+        kept=1,
+    )
+    idx, gate, _ = lax.optimization_barrier((idx, gate, summed))
+    place, slots, names = call(
+        place_kernel,
+        [
+            shape((LANES + experts, experts * BLOCK)), shape((experts, LANES), F32),
+            shape((top, LANES), jnp.int32),
+        ],
+        experts * BLOCK * LANES * 8, (idx, gate),
     )
     back = lax.all_to_all(
         back.reshape(experts, BLOCK, LANES), GROUP, split_axis=0, concat_axis=0, tiled=True
@@ -341,7 +377,7 @@
     acts_grad, gate_grad = call(
         token_kernel, [shape((tokens, width)), shape((top, tokens))],
         4 * experts * BLOCK * LANES * LANES,
-        (idx, gate, back.reshape(experts * BLOCK, LANES)),
+        (place, slots, names, gate, back.reshape(experts * BLOCK, LANES)),
     )
     return (acts_grad, gate_grad.T, wg_grad[None], wu_grad[None], wd_grad[None])
 

time: 130 us -> 128 us (0.985)
    pallas_call x8 -> x10, Pallas kernels: 14.6 us -> 14.3 us  [call(): pl.pallas_call(kernel, out_shape=outs, in_specs=[SMEM] * scalars + [space...]
where the time goes in v3:
time: 128 us
  blocking collectives  48.5 us (38%)
  waiting for transfers between devices  39.4 us (31%)
  starting transfers between devices  24.3 us (19%)
  Pallas kernels  14.3 us (11%)
    all_to_all x1, blocking collectives, body(): lax.all_to_all(send.reshape(experts, lines, LANES), GROUP, split_axis=0,...  48.5 us
    ppermute x6, waiting for transfers between devices, swap(): lax.ppermute(x, 'rep', [(i, i ^ bit) for i in range(lax.axis_size('rep'))])  22.9 us
    ppermute x6, starting transfers between devices, swap(): lax.ppermute(x, 'rep', [(i, i ^ bit) for i in range(lax.axis_size('rep'))])  16.5 us
    all_to_all x1, waiting for transfers between devices, body(): lax.all_to_all(back.reshape(experts, BLOCK, LANES), GROUP, split_axis=0,...  16.5 us
    pallas_call x10, Pallas kernels, call(): pl.pallas_call(kernel, out_shape=outs, in_specs=[SMEM] * scalars + [space...  14.3 us
    all_to_all x1, starting transfers between devices, body(): lax.all_to_all(back.reshape(experts, BLOCK, LANES), GROUP, split_axis=0,...  7.74 us
  transfers between devices with their start and end apart: 7, of which 4 were waited for; matrix products, arithmetic and copies ran while one was open for 0% of the time, Pallas kernels for 6%

profile of v3, /device:TPU:1, one launch (start us, length us, event | category | flops | bytes accessed | tf_op | source)
XLA Modules:
  0.0 127.7 jit_solution(16828048197335038672)
XLA Ops:
  0.6 2.5 %shard_map.110 = bf16[3072,128]{1,0:T(8,128)(2,1)} custom-call(s32[8,32]{1,0:T(8,128)} %bitcast.30, bf16[8,32]{1,0:T(8,128)(2,1)} %bitcast.27, bf16[32,512]{1,0:T(8,128)(2,1)} %refs_2_.1, bf16[32,512]{1,0:T(8,128)(2,1)} %refs_3_.1), custom_call_target="tpu_custom_call" | custom-call | flops 201326592 | bytes 853504 | tf_op jit(solution)/shard_map/pallas_call | solution.py:287
  3.2 0.0 copy-start.2
  3.2 48.5 %all_to_all.10 = bf16[128,24,128]{2,1,0:T(8,128)(2,1)S(1)} all-to-all(bf16[128,24,128]{2,1,0:T(8,128)(2,1)} %bitcast.32), channel_id=1, replica_groups=mesh['ctx'=8,'exp'=16,'rep'=4] {'ctx','exp'}, dimensions={0} | all-to-all | bytes 1572864 | tf_op jit(solution)/shard_map/all_to_all | solution.py:329
  51.7 0.0 copy-start
  51.7 0.0 copy-start.1
  51.7 0.6 shard_map.111.own_ref
  52.3 1.9 %collective-permute-start = (bf16[384,1024]{1,0:T(8,128)(2,1)S(1)}, bf16[384,1024]{1,0:T(8,128)(2,1)}, u32[]{:S(2)}, u32[]{:S(2)}) collective-permute-start(bf16[384,1024]{1,0:T(8,128)(2,1)S(1)} %shard_map.111.own_ref), channel_id=1, source_target_pairs={{0,2},{1,3},{2,0},{3,1},{4,6},{5,7},{6,4},{7,5},{8,10},{9,11},{10,... | collective-permute-start | bytes 2359304 | tf_op jit(solution)/shard_map/ppermute | solution.py:19
  54.2 3.6 %collective-permute-start.2 = (bf16[384,1024]{1,0:T(8,128)(2,1)S(1)}, bf16[384,1024]{1,0:T(8,128)(2,1)}, u32[]{:S(2)}, u32[]{:S(2)}) collective-permute-start(bf16[384,1024]{1,0:T(8,128)(2,1)S(1)} %shard_map.111.own_ref), channel_id=1, source_target_pairs={{0,1},{1,0},{2,3},{3,2},{4,5},{5,4},{6,7},{7,6},{8,9},{9,8},{10,11... | collective-permute-start | bytes 2359304 | tf_op jit(solution)/shard_map/ppermute | solution.py:19
  57.8 0.0 copy-done.2
  57.8 0.0 copy-done
  57.8 0.0 copy-done.1
  57.8 0.5 shard_map.112
  58.3 13.3 %collective-permute-done.chip_ref = bf16[384,1024]{1,0:T(8,128)(2,1)} collective-permute-done((bf16[384,1024]{1,0:T(8,128)(2,1)S(1)}, bf16[384,1024]{1,0:T(8,128)(2,1)}, u32[]{:S(2)}, u32[]{:S(2)}) %collective-permute-start) | collective-permute-done | bytes 786464 | tf_op jit(solution)/shard_map/ppermute | solution.py:19
  71.6 4.5 %collective-permute-start.1 = (bf16[384,1024]{1,0:T(8,128)(2,1)}, bf16[384,1024]{1,0:T(8,128)(2,1)S(1)}, u32[]{:S(2)}, u32[]{:S(2)}) collective-permute-start(bf16[384,1024]{1,0:T(8,128)(2,1)} %collective-permute-done.chip_ref), channel_id=1, source_target_pairs={{0,1},{1,0},{2,3},{3,2},{4,5},{5,4},{6,7},{7,6},{8,9},{9,8},{10,11... | collective-permute-start | bytes 2359304 | tf_op jit(solution)/shard_map/ppermute | solution.py:19
  76.1 0.0 collective-permute-done.2.core_ref
  76.1 2.2 %shard_map.113 = (f32[384,192]{1,0:T(8,128)S(1)}, f32[384,192]{1,0:T(8,128)S(1)}, f32[384,192]{1,0:T(8,128)S(1)}) custom-call(s32[1]{0:T(128)} %bitcast.2.me_ref, bf16[384,1024]{1,0:T(8,128)(2,1)} %collective-permute-done.2.core_ref, bf16[384,1024]{1,0:T(8,128)(2,1)} %collective-permute-done.chip_ref, bf16[192,2048]{1,0:T(8,128)(2,1)S(1)} %bitcast.15, ...), custom_call_target="tpu_custom_call" | custom-call | flops 452984832 | bytes 5701636 | tf_op jit(solution)/shard_map/pallas_call | solution.py:287
  78.3 0.0 collective-permute-done.1.far_ref
  78.3 0.0 copy-start.3
  78.4 1.1 shard_map.114
  79.5 0.0 copy-done.3
  79.5 0.0 copy-start.5
  79.5 2.2 %collective-permute-start.3 = (bf16[416,512]{1,0:T(8,128)(2,1)S(1)}, bf16[416,512]{1,0:T(8,128)(2,1)S(1)}, u32[]{:S(2)}, u32[]{:S(2)}) collective-permute-start(bf16[416,512]{1,0:T(8,128)(2,1)S(1)} %get-tuple-element.48), channel_id=1, source_target_pairs={{0,1},{1,0},{2,3},{3,2},{4,5},{5,4},{6,7},{7,6},{8,9},{9,8},{10,11... | collective-permute-start | bytes 1277960 | tf_op jit(solution)/shard_map/ppermute | solution.py:19
  81.7 1.5 %collective-permute-done.3 = bf16[416,512]{1,0:T(8,128)(2,1)S(1)} collective-permute-done((bf16[416,512]{1,0:T(8,128)(2,1)S(1)}, bf16[416,512]{1,0:T(8,128)(2,1)S(1)}, u32[]{:S(2)}, u32[]{:S(2)}) %collective-permute-start.3) | collective-permute-done | bytes 426016 | tf_op jit(solution)/shard_map/ppermute | solution.py:19
  83.1 0.1 add.6
  83.3 0.0 copy-done.5
  83.3 1.9 %collective-permute-start.4 = (bf16[416,512]{1,0:T(8,128)(2,1)S(1)}, bf16[416,512]{1,0:T(8,128)(2,1)S(1)}, u32[]{:S(2)}, u32[]{:S(2)}) collective-permute-start(bf16[416,512]{1,0:T(8,128)(2,1)S(1)} %add.6), channel_id=1, source_target_pairs={{0,2},{1,3},{2,0},{3,1},{4,6},{5,7},{6,4},{7,5},{8,10},{9,11},{10,... | collective-permute-start | bytes 1277960 | tf_op jit(solution)/shard_map/ppermute | solution.py:19
  85.2 0.6 shard_map.115
  85.8 2.5 %collective-permute-start.5 = (bf16[416,512]{1,0:T(8,128)(2,1)S(1)}, bf16[416,512]{1,0:T(8,128)(2,1)S(1)}, u32[]{:S(2)}, u32[]{:S(2)}) collective-permute-start(bf16[416,512]{1,0:T(8,128)(2,1)S(1)} %get-tuple-element.54), channel_id=1, source_target_pairs={{0,1},{1,0},{2,3},{3,2},{4,5},{5,4},{6,7},{7,6},{8,9},{9,8},{10,11... | collective-permute-start | bytes 1277960 | tf_op jit(solution)/shard_map/ppermute | solution.py:19
  88.2 8.1 %collective-permute-done.4 = bf16[416,512]{1,0:T(8,128)(2,1)S(1)} collective-permute-done((bf16[416,512]{1,0:T(8,128)(2,1)S(1)}, bf16[416,512]{1,0:T(8,128)(2,1)S(1)}, u32[]{:S(2)}, u32[]{:S(2)}) %collective-permute-start.4) | collective-permute-done | bytes 426016 | tf_op jit(solution)/shard_map/ppermute | solution.py:19
  96.3 0.1 add.7.sum_ref
  96.4 0.0 collective-permute-done.5.core_ref
  96.5 1.2 shard_map.117
  97.6 0.0 copy-start.4
  97.7 0.0 copy-start.6
  97.7 7.7 %all-to-all-start.1 = ((bf16[128,16,128]{2,1,0:T(8,128)(2,1)}), bf16[128,16,128]{2,1,0:T(8,128)(2,1)S(1)}, u32[]{:S(2)}, u32[]{:S(2)}) async-start(bf16[128,16,128]{2,1,0:T(8,128)(2,1)} %bitcast.8), calls=%async_computation.1 | async-start | bytes 1048576 | tf_op jit(solution)/shard_map/all_to_all | solution.py:374
  105.4 0.0 copy-done.4
  105.4 0.0 copy-done.6
  105.4 0.0 copy-start.7
  105.4 0.0 copy-start.8
  105.5 4.0 %shard_map.119 = (bf16[192,2048]{1,0:T(8,128)(2,1)}, bf16[192,2048]{1,0:T(8,128)(2,1)}, bf16[192,2048]{1,0:T(8,128)(2,1)}) custom-call(s32[1]{0:T(128)} %bitcast.2.me_ref, bf16[384,1024]{1,0:T(8,128)(2,1)S(1)} %shard_map.111.own_ref, bf16[384,1024]{1,0:T(8,128)(2,1)} %collective-permute-done.2.core_ref, bf16[384,1024]{1,0:T(8,128)(2,1)} %collective-permute-done.chip_ref, ...), custom_call_target="tpu_custom_call" | custom-call | flops 905969664 | bytes 5947396 | tf_op jit(solution)/shard_map/pallas_call | solution.py:287
  109.4 0.0 copy-done.7
  109.5 0.0 copy-done.8
  109.5 0.6 shard_map.116
  110.0 16.5 %all-to-all-done.1 = bf16[128,16,128]{2,1,0:T(8,128)(2,1)S(1)} async-done(((bf16[128,16,128]{2,1,0:T(8,128)(2,1)}), bf16[128,16,128]{2,1,0:T(8,128)(2,1)S(1)}, u32[]{:S(2)}, u32[]{:S(2)}) %all-to-all-start.1) | async-done | bytes 524320 | tf_op jit(solution)/shard_map/all_to_all | solution.py:374
  126.5 1.2 shard_map.118
Async XLA Ops:
  3.2 54.7 %copy-start.2 = (bf16[1,192,2048]{2,1,0:T(8,128)(2,1)S(1)}, bf16[1,192,2048]{2,1,0:T(8,128)(2,1)}, u32[]{:S(2)}) copy-start(bf16[1,192,2048]{2,1,0:T(8,128)(2,1)} %param.13) | copy-start | bytes 2359300
  51.7 6.2 %copy-start = (bf16[1,192,2048]{2,1,0:T(8,128)(2,1)S(1)}, bf16[1,192,2048]{2,1,0:T(8,128)(2,1)}, u32[]{:S(2)}) copy-start(bf16[1,192,2048]{2,1,0:T(8,128)(2,1)} %param.11) | copy-start | bytes 2359300
  51.7 6.2 %copy-start.1 = (bf16[1,192,2048]{2,1,0:T(8,128)(2,1)S(1)}, bf16[1,192,2048]{2,1,0:T(8,128)(2,1)}, u32[]{:S(2)}) copy-start(bf16[1,192,2048]{2,1,0:T(8,128)(2,1)} %param.12) | copy-start | bytes 2359300
  52.3 19.4 %collective-permute-start = (bf16[384,1024]{1,0:T(8,128)(2,1)S(1)}, bf16[384,1024]{1,0:T(8,128)(2,1)}, u32[]{:S(2)}, u32[]{:S(2)}) collective-permute-start(bf16[384,1024]{1,0:T(8,128)(2,1)S(1)} %shard_map.111.own_ref), channel_id=1, source_target_pairs={{0,2},{1,3},{2,0},{3,1},{4,6},{5,7},{6,4},{7,5},{8,10},{9,11},{10,... | collective-permute-start | bytes 2359304 | tf_op jit(solution)/shard_map/ppermute | solution.py:19
  54.2 21.9 %collective-permute-start.2 = (bf16[384,1024]{1,0:T(8,128)(2,1)S(1)}, bf16[384,1024]{1,0:T(8,128)(2,1)}, u32[]{:S(2)}, u32[]{:S(2)}) collective-permute-start(bf16[384,1024]{1,0:T(8,128)(2,1)S(1)} %shard_map.111.own_ref), channel_id=1, source_target_pairs={{0,1},{1,0},{2,3},{3,2},{4,5},{5,4},{6,7},{7,6},{8,9},{9,8},{10,11... | collective-permute-start | bytes 2359304 | tf_op jit(solution)/shard_map/ppermute | solution.py:19
  71.6 6.7 %collective-permute-start.1 = (bf16[384,1024]{1,0:T(8,128)(2,1)}, bf16[384,1024]{1,0:T(8,128)(2,1)S(1)}, u32[]{:S(2)}, u32[]{:S(2)}) collective-permute-start(bf16[384,1024]{1,0:T(8,128)(2,1)} %collective-permute-done.chip_ref), channel_id=1, source_target_pairs={{0,1},{1,0},{2,3},{3,2},{4,5},{5,4},{6,7},{7,6},{8,9},{9,8},{10,11... | collective-permute-start | bytes 2359304 | tf_op jit(solution)/shard_map/ppermute | solution.py:19
  78.3 1.1 copy-start.3
  79.5 3.8 %copy-start.5 = (bf16[384,192]{1,0:T(8,128)(2,1)}, bf16[384,192]{1,0:T(8,128)(2,1)S(1)}, u32[]{:S(2)}) copy-start(bf16[384,192]{1,0:T(8,128)(2,1)S(1)} %get-tuple-element.57.hid_ref) | copy-start | bytes 442372
  79.5 3.7 %collective-permute-start.3 = (bf16[416,512]{1,0:T(8,128)(2,1)S(1)}, bf16[416,512]{1,0:T(8,128)(2,1)S(1)}, u32[]{:S(2)}, u32[]{:S(2)}) collective-permute-start(bf16[416,512]{1,0:T(8,128)(2,1)S(1)} %get-tuple-element.48), channel_id=1, source_target_pairs={{0,1},{1,0},{2,3},{3,2},{4,5},{5,4},{6,7},{7,6},{8,9},{9,8},{10,11... | collective-permute-start | bytes 1277960 | tf_op jit(solution)/shard_map/ppermute | solution.py:19
  83.3 13.1 %collective-permute-start.4 = (bf16[416,512]{1,0:T(8,128)(2,1)S(1)}, bf16[416,512]{1,0:T(8,128)(2,1)S(1)}, u32[]{:S(2)}, u32[]{:S(2)}) collective-permute-start(bf16[416,512]{1,0:T(8,128)(2,1)S(1)} %add.6), channel_id=1, source_target_pairs={{0,2},{1,3},{2,0},{3,1},{4,6},{5,7},{6,4},{7,5},{8,10},{9,11},{10,... | collective-permute-start | bytes 1277960 | tf_op jit(solution)/shard_map/ppermute | solution.py:19
  85.8 10.7 %collective-permute-start.5 = (bf16[416,512]{1,0:T(8,128)(2,1)S(1)}, bf16[416,512]{1,0:T(8,128)(2,1)S(1)}, u32[]{:S(2)}, u32[]{:S(2)}) collective-permute-start(bf16[416,512]{1,0:T(8,128)(2,1)S(1)} %get-tuple-element.54), channel_id=1, source_target_pairs={{0,1},{1,0},{2,3},{3,2},{4,5},{5,4},{6,7},{7,6},{8,9},{9,8},{10,11... | collective-permute-start | bytes 1277960 | tf_op jit(solution)/shard_map/ppermute | solution.py:19
  97.6 7.8 %copy-start.4 = (bf16[384,1024]{1,0:T(8,128)(2,1)S(1)}, bf16[384,1024]{1,0:T(8,128)(2,1)}, u32[]{:S(2)}) copy-start(bf16[384,1024]{1,0:T(8,128)(2,1)} %copy-done.3) | copy-start | bytes 2359300
  97.7 7.8 %copy-start.6 = (bf16[384,192]{1,0:T(8,128)(2,1)S(1)}, bf16[384,192]{1,0:T(8,128)(2,1)}, u32[]{:S(2)}) copy-start(bf16[384,192]{1,0:T(8,128)(2,1)} %copy-done.5) | copy-start | bytes 442372
  97.7 28.8 %all-to-all-start.1 = ((bf16[128,16,128]{2,1,0:T(8,128)(2,1)}), bf16[128,16,128]{2,1,0:T(8,128)(2,1)S(1)}, u32[]{:S(2)}, u32[]{:S(2)}) async-start(bf16[128,16,128]{2,1,0:T(8,128)(2,1)} %bitcast.8), calls=%async_computation.1 | async-start | bytes 1048576 | tf_op jit(solution)/shard_map/all_to_all | solution.py:374
  105.4 4.0 %copy-start.7 = (bf16[32,8]{0,1:T(8,128)(2,1)S(1)}, bf16[32,8]{0,1:T(8,128)(2,1)}, u32[]{:S(2)}) copy-start(bf16[32,8]{0,1:T(8,128)(2,1)} %param.10) | copy-start | bytes 1540
  105.4 4.0 %copy-start.8 = (s32[32,8]{0,1:T(8,128)S(1)}, s32[32,8]{0,1:T(8,128)}, u32[]{:S(2)}) copy-start(s32[32,8]{0,1:T(8,128)} %param.9) | copy-start | bytes 3076
